TPU v7x, 32 devices: a whole 2x2x4 slice. The times are simulated.
32 devices in a mesh: seq: 8 (over z, core), dp: 4 (over y, x).
Axes of the slice: x: 2, y: 2, z: 4, core: 2. Of those that a mesh axis runs over, the one named last changes fastest.
Arguments:
- block_input: bfloat16 [32, 1024, 768], P('dp', 'seq'), may hold values from -6 to 6
- doc_bounds: int32 [32, 2], P('dp'), may hold values from 1 to 1024, as said below
- first_gain: bfloat16 [768], P('dp'), may hold values from 0.5 to 1.5
- first_shift: bfloat16 [768], P('dp'), may hold values from -1 to 1
- qkv_weight: bfloat16 [768, 2304], P('dp'), may hold values from -0.21875 to 0.21875
- qv_bias: bfloat16 [1536], P('dp'), may hold values from -1 to 1
- score_weight: bfloat16 [768, 12], P('dp'), may hold values from -0.3125 to 0.3125
- out_weight: bfloat16 [768, 768], P('dp'), may hold values from -0.625 to 0.625
- out_bias: bfloat16 [768], P('dp'), may hold values from -1 to 1
- second_gain: bfloat16 [768], P('dp'), may hold values from 0.5 to 1.5
- second_shift: bfloat16 [768], P('dp'), may hold values from -1 to 1
- fc_weight: bfloat16 [768, 3072], P('dp'), may hold values from -0.21875 to 0.21875
- fc_bias: bfloat16 [3072], P('dp'), may hold values from -1 to 1
- down_weight: bfloat16 [3072, 768], P('dp'), may hold values from -0.21875 to 0.21875
- down_bias: bfloat16 [768], P('dp'), may hold values from -1 to 1
- cotangent: bfloat16 [32, 1024, 768], P('dp', 'seq'), may hold values from -6 to 6
Outputs:
- block_output: bfloat16 [32, 1024, 768], P('dp', 'seq')
- input_grad: float32 [32, 1024, 768], P('dp', 'seq')
- first_gain_grad: float32 [768], P('dp')
- first_shift_grad: float32 [768], P('dp')
- qkv_weight_grad: float32 [768, 2304], P('dp')
- qv_bias_grad: float32 [1536], P('dp')
- score_weight_grad: float32 [768, 12], P('dp')
- out_weight_grad: float32 [768, 768], P('dp')
- out_bias_grad: float32 [768], P('dp')
- second_gain_grad: float32 [768], P('dp')
- second_shift_grad: float32 [768], P('dp')
- fc_weight_grad: float32 [768, 3072], P('dp')
- fc_bias_grad: float32 [3072], P('dp')
- down_weight_grad: float32 [3072, 768], P('dp')
- down_bias_grad: float32 [768], P('dp')
Inputs may be any that keep to these rules, and one draw needn't show every extreme that they name: `doc_bounds`: the first entry of a row is the start of its second document, below 128; the second entry is the start of its third document, above 896, or 1024 where the row holds two documents.
All inputs are finite; a program needn't handle non-finite values.
Results may differ from a plain program's by a relative error of at most 0.018.
Values may be sent and summed in bfloat16 or wider, within the bound.
No kernel may reach another device: no remote copies, remote signals or barrier semaphores. Data moves between devices by JAX's collectives and lax.ppermute only.
A program may use at most 192 MiB of HBM per device.

v0:
```python
from functools import partial
import math

import jax
import jax.numpy as jnp
from jax import lax
from jax.sharding import PartitionSpec as P

KTOP = 64
WINDOW = 64
MB = 2


EPSILON = 1e-05
HIGH = lax.Precision.HIGHEST
NEGATIVE = -1e30


def prefix(value, axis, join, neutral, backward):
    count, mine = (lax.axis_size(axis), lax.axis_index(axis))
    pieces = jax.tree.map(lambda part: lax.all_gather(part, axis), value)
    if backward:
        pieces = jax.tree.map(lambda part: part[::-1], pieces)
        mine = count - 1 - mine
    running = jax.tree.map(
        lambda part, zero: jnp.full_like(part, 0) + jnp.asarray(zero, part.dtype), value, neutral
    )

    def hop(position, running):
        longer = join(running, jax.tree.map(lambda part: part[position], pieces))
        return jax.tree.map(lambda new, old: jnp.where(position < mine, new, old), longer, running)

    return lax.fori_loop(0, count - 1, hop, running)


def from_behind(value, axis, steps):
    count = lax.axis_size(axis)
    leading, last = (max(0, -steps), min(count, count - steps))
    return lax.ppermute(value, axis, [(source, source + steps) for source in range(leading, last)])


def layer_norm(values, norm_gain, norm_shift):
    average = jnp.mean(values, axis=-1, keepdims=True)
    centred = values - average
    variance = jnp.mean(centred * centred, axis=-1, keepdims=True)
    return centred * lax.rsqrt(variance + EPSILON) * norm_gain + norm_shift


def segment_at(places, bounds):
    return (places[None, :] >= bounds[:, 0:1]).astype(jnp.int32) + (
        places[None, :] >= bounds[:, 1:2]
    ).astype(jnp.int32)


def prefix_combine(earlier, later):
    peak_a, total_a, reset_a = earlier
    peak_b, total_b, reset_b = later
    joined = jnp.maximum(peak_a, peak_b)
    merged = total_a * jnp.exp(peak_a - joined) + total_b * jnp.exp(peak_b - joined)
    restart = reset_b > 0.5
    return (
        jnp.where(restart, peak_b, joined),
        jnp.where(restart, total_b, merged),
        jnp.maximum(reset_a, reset_b),
    )


def suffix_combine(earlier, later):
    total_a, reset_a = earlier
    total_b, reset_b = later
    return (jnp.where(reset_b > 0.5, total_b, total_b + total_a), jnp.maximum(reset_a, reset_b))


def body(
    block_input,
    doc_bounds,
    first_gain,
    first_shift,
    qkv_weight,
    qv_bias,
    score_weight,
    out_weight,
    out_bias,
    second_gain,
    second_shift,
    fc_weight,
    fc_bias,
    down_weight,
    down_bias,
    cotangent,
):
    seq_count, blocks, width = block_input.shape
    per_batch = seq_count // MB
    heads = score_weight.shape[1]
    head_dim = width // heads
    window = WINDOW
    scale = 1.0 / math.sqrt(head_dim)
    start = lax.axis_index("seq") * blocks
    finish = start + blocks - 1
    position = start + jnp.arange(blocks, dtype=jnp.int32)
    key_position = start - window + jnp.arange(window + blocks, dtype=jnp.int32)
    distance = position[:, None] - key_position[None, :]
    in_block = jnp.arange(window + blocks)[None, :] >= window
    base_allowed = (distance >= 0) & (key_position[None, :] >= 0) & ((distance < window) | in_block)
    inner_window = distance[:, window:] < window
    causal = jnp.arange(blocks)[None, :] <= jnp.arange(blocks)[:, None]
    gelu_tanh = partial(jax.nn.gelu, approximate=True)

    def make_logits(queries, keys_all, importance, threshold, allowed):
        raw = jnp.einsum("sihd,sjhd->shij", queries, keys_all, preferred_element_type=jnp.float32)
        difference = (
            jnp.transpose(threshold, (0, 2, 1))[:, :, :, None]
            - jnp.transpose(importance, (0, 2, 1))[:, :, None, :]
        )
        gated = jnp.where(inner_window, 0.0, -jax.nn.softplus(difference))
        bias_all = jnp.concatenate(
            [jnp.zeros(gated.shape[:3] + (window,), jnp.float32), gated], axis=-1
        )
        return (jnp.where(allowed, raw * scale + bias_all, NEGATIVE), difference)

    def run_backward(weights, kept, bounds, grad_out):
        (
            g_first,
            s_first,
            w_qkv,
            b_qv,
            w_score,
            w_out,
            b_out,
            g_second,
            s_second,
            w_fc,
            b_fc,
            w_down,
            b_down,
        ) = weights
        (
            flat_in,
            normed,
            queries,
            keys_all,
            values_all,
            importance,
            threshold,
            log_total,
            attended,
            middle,
            second,
            pre_act,
            hidden,
            allowed,
            lower,
            segment,
        ) = kept
        seq_here = queries.shape[0]
        row_count = seq_here * blocks
        dy_low = grad_out.reshape(row_count, width)
        dy_full = dy_low.astype(jnp.float32)
        grad_w_down = jnp.einsum("nf,nd->fd", hidden, dy_low, preferred_element_type=jnp.float32)
        grad_b_down = jnp.sum(dy_full, axis=0)
        d_hidden = jnp.einsum("nd,fd->nf", dy_low, w_down, preferred_element_type=jnp.float32)
        gelu_back = jax.vjp(gelu_tanh, pre_act)[1]
        d_pre = gelu_back(d_hidden)[0].astype(jnp.bfloat16)
        grad_w_fc = jnp.einsum("nd,nf->df", second, d_pre, preferred_element_type=jnp.float32)
        grad_b_fc = jnp.sum(d_pre.astype(jnp.float32), axis=0)
        d_second = jnp.einsum("nf,df->nd", d_pre, w_fc, preferred_element_type=jnp.float32)
        second_back = jax.vjp(
            layer_norm, middle, g_second.astype(jnp.float32), s_second.astype(jnp.float32)
        )[1]
        d_middle_norm, grad_g_second, grad_s_second = second_back(d_second)
        d_middle = dy_full + d_middle_norm
        d_branch = d_middle.astype(jnp.bfloat16)
        grad_w_out = jnp.einsum("nd,ne->de", attended, d_branch, preferred_element_type=jnp.float32)
        grad_b_out = jnp.sum(d_branch.astype(jnp.float32), axis=0)
        d_attended = jnp.einsum(
            "ne,de->nd", d_branch, w_out, preferred_element_type=jnp.float32
        ).astype(jnp.bfloat16)
        d_attended = d_attended.reshape(seq_here, blocks, heads, head_dim)
        logits, difference = make_logits(queries, keys_all, importance, threshold, allowed)
        probs = jnp.exp(logits - log_total)
        probs_low = probs.astype(jnp.bfloat16)
        d_probs = jnp.einsum(
            "sihd,sjhd->shij", d_attended, values_all, preferred_element_type=jnp.float32
        )
        d_values_all = jnp.einsum(
            "shij,sihd->sjhd", probs_low, d_attended, preferred_element_type=jnp.float32
        )
        d_logits = probs * (d_probs - jnp.sum(probs * d_probs, axis=-1, keepdims=True))
        d_raw = (d_logits * scale).astype(jnp.bfloat16)
        d_queries = jnp.einsum(
            "shij,sjhd->sihd", d_raw, keys_all, preferred_element_type=jnp.float32
        )
        d_keys_all = jnp.einsum(
            "shij,sihd->sjhd", d_raw, queries, preferred_element_type=jnp.float32
        )
        gate_term = jnp.where(
            inner_window, 0.0, d_logits[..., window:] * jax.nn.sigmoid(difference)
        )
        d_threshold = -jnp.transpose(jnp.sum(gate_term, axis=-1), (0, 2, 1))
        d_importance = jnp.transpose(jnp.sum(gate_term, axis=2), (0, 2, 1))
        weighted = d_threshold * jnp.exp(-threshold) / KTOP
        local_after = jnp.einsum("sij,sih->sjh", lower, weighted, precision=HIGH)
        first_part = (segment == segment[:, :1]).astype(jnp.float32)[:, :, None]
        first_total = jnp.sum(weighted * first_part, axis=1)
        first_b = bounds[:, 0:1]
        second_b = bounds[:, 1:2]
        restart_back = jnp.broadcast_to(
            (
                (first_b > start) & (first_b <= finish + 1)
                | (second_b > start) & (second_b <= finish + 1)
            ).astype(jnp.float32),
            first_total.shape,
        )
        after_total, after_flag = prefix(
            (first_total, restart_back),
            "seq",
            suffix_combine,
            (jnp.zeros_like(first_total), jnp.zeros_like(first_total)),
            True,
        )
        following = segment_at(jnp.reshape(finish + 1, (1,)), bounds)
        continues_back = (segment == following).astype(jnp.float32)[:, :, None]
        d_importance = d_importance + jnp.exp(importance) * (
            local_after + continues_back * after_total[:, None]
        )
        back_keys, back_values = (
            from_behind(d_keys_all[:, :window].astype(jnp.bfloat16), "seq", -1).astype(jnp.float32),
            from_behind(d_values_all[:, :window].astype(jnp.bfloat16), "seq", -1).astype(
                jnp.float32
            ),
        )
        pad_zero = jnp.zeros((seq_here, blocks - window, heads, head_dim), jnp.float32)
        d_keys = d_keys_all[:, window:] + jnp.concatenate([pad_zero, back_keys], axis=1)
        d_values = d_values_all[:, window:] + jnp.concatenate([pad_zero, back_values], axis=1)
        d_qkv = jnp.concatenate(
            [
                d_queries.reshape(row_count, width),
                d_keys.reshape(row_count, width),
                d_values.reshape(row_count, width),
            ],
            axis=1,
        ).astype(jnp.bfloat16)
        grad_w_qkv = jnp.einsum("nd,ne->de", normed, d_qkv, preferred_element_type=jnp.float32)
        column_sums = jnp.sum(d_qkv.astype(jnp.float32), axis=0)
        grad_b_qv = jnp.concatenate([column_sums[:width], column_sums[2 * width :]])
        flat_importance = d_importance.reshape(row_count, heads)
        grad_w_score = jnp.einsum(
            "nd,nh->dh", normed.astype(jnp.float32), flat_importance, precision=HIGH
        )
        d_normed = jnp.einsum("ne,de->nd", d_qkv, w_qkv, preferred_element_type=jnp.float32)
        d_normed = d_normed + jnp.einsum(
            "nh,dh->nd", flat_importance, w_score.astype(jnp.float32), precision=HIGH
        )
        first_back = jax.vjp(
            layer_norm, flat_in, g_first.astype(jnp.float32), s_first.astype(jnp.float32)
        )[1]
        d_input_norm, grad_g_first, grad_s_first = first_back(d_normed)
        d_input = (d_middle + d_input_norm).reshape(seq_here, blocks, width)
        grads = (
            grad_g_first,
            grad_s_first,
            grad_w_qkv,
            grad_b_qv,
            grad_w_score,
            grad_w_out,
            grad_b_out,
            grad_g_second,
            grad_s_second,
            grad_w_fc,
            grad_b_fc,
            grad_w_down,
            grad_b_down,
        )
        return (d_input, grads)

    results = []
    kept_all = []
    held = []
    for batch in range(MB):
        inputs = block_input[batch * per_batch : (batch + 1) * per_batch]
        bounds = doc_bounds[batch * per_batch : (batch + 1) * per_batch]
        whole = (
            lax.all_gather(first_gain, "dp", axis=0, tiled=True),
            lax.all_gather(first_shift, "dp", axis=0, tiled=True),
            lax.all_gather(qkv_weight, "dp", axis=0, tiled=True),
            lax.all_gather(qv_bias, "dp", axis=0, tiled=True),
            lax.all_gather(score_weight, "dp", axis=0, tiled=True),
            lax.all_gather(out_weight, "dp", axis=0, tiled=True),
            lax.all_gather(out_bias, "dp", axis=0, tiled=True),
            lax.all_gather(second_gain, "dp", axis=0, tiled=True),
            lax.all_gather(second_shift, "dp", axis=0, tiled=True),
            lax.all_gather(fc_weight, "dp", axis=0, tiled=True),
            lax.all_gather(fc_bias, "dp", axis=0, tiled=True),
            lax.all_gather(down_weight, "dp", axis=0, tiled=True),
            lax.all_gather(down_bias, "dp", axis=0, tiled=True),
        )
        (
            run_g_first,
            run_s_first,
            run_w_qkv,
            run_b_qv,
            run_w_score,
            run_w_out,
            run_b_out,
            run_g_second,
            run_s_second,
            run_w_fc,
            run_b_fc,
            run_w_down,
            run_b_down,
        ) = whole
        run_seq_here = inputs.shape[0]
        run_row_count = run_seq_here * blocks
        run_flat_in = inputs.reshape(run_row_count, width).astype(jnp.float32)
        run_normed = layer_norm(run_flat_in, run_g_first, run_s_first).astype(jnp.bfloat16)
        full_bias = jnp.concatenate(
            [run_b_qv[:width], jnp.zeros((width,), run_b_qv.dtype), run_b_qv[width:]]
        ).astype(jnp.float32)
        projected = (
            jnp.dot(run_normed, run_w_qkv, preferred_element_type=jnp.float32) + full_bias
        ).astype(jnp.bfloat16)
        run_queries = projected[:, :width].reshape(run_seq_here, blocks, heads, head_dim)
        keys = projected[:, width : 2 * width].reshape(run_seq_here, blocks, heads, head_dim)
        values = projected[:, 2 * width :].reshape(run_seq_here, blocks, heads, head_dim)
        run_importance = jnp.dot(
            run_normed, run_w_score, preferred_element_type=jnp.float32
        ).reshape(run_seq_here, blocks, heads)
        run_segment = segment_at(position, bounds)
        key_segment = segment_at(key_position, bounds)
        run_allowed = (base_allowed[None] & (run_segment[:, :, None] == key_segment[:, None, :]))[
            :, None
        ]
        run_lower = (causal[None] & (run_segment[:, :, None] == run_segment[:, None, :])).astype(
            jnp.float32
        )
        peak = jnp.max(run_importance, axis=1)
        scaled = jnp.exp(run_importance - peak[:, None])
        local = jnp.einsum("sij,sjh->sih", run_lower, scaled, precision=HIGH)
        last_part = (run_segment == run_segment[:, -1:]).astype(jnp.float32)[:, :, None]
        block_total = jnp.sum(scaled * last_part, axis=1)
        run_first_b = bounds[:, 0:1]
        run_second_b = bounds[:, 1:2]
        restart = jnp.broadcast_to(
            (
                (run_first_b >= start) & (run_first_b <= finish)
                | (run_second_b >= start) & (run_second_b <= finish)
            ).astype(jnp.float32),
            peak.shape,
        )
        carry_peak, carry_total, carry_flag = prefix(
            (peak, block_total, restart),
            "seq",
            prefix_combine,
            (jnp.full_like(peak, NEGATIVE), jnp.zeros_like(peak), jnp.zeros_like(peak)),
            False,
        )
        before = segment_at(jnp.reshape(start - 1, (1,)), bounds)
        continues = (run_segment == before).astype(jnp.float32)[:, :, None]
        joined = jnp.maximum(peak, carry_peak)
        mass = (
            local * jnp.exp(peak - joined)[:, None]
            + continues * (carry_total * jnp.exp(carry_peak - joined))[:, None]
        )
        run_threshold = joined[:, None] + jnp.log(mass) - math.log(KTOP)
        got_keys, got_values = from_behind(
            (keys[:, blocks - window :], values[:, blocks - window :]), "seq", 1
        )
        run_keys_all = jnp.concatenate([got_keys, keys], axis=1)
        run_values_all = jnp.concatenate([got_values, values], axis=1)
        run_logits, run_difference = make_logits(
            run_queries, run_keys_all, run_importance, run_threshold, run_allowed
        )
        peak_row = jnp.max(run_logits, axis=-1, keepdims=True)
        expd = jnp.exp(run_logits - peak_row)
        denominator = jnp.sum(expd, axis=-1, keepdims=True)
        run_probs = expd / denominator
        run_log_total = peak_row + jnp.log(denominator)
        run_attended = jnp.einsum(
            "shij,sjhd->sihd",
            run_probs.astype(jnp.bfloat16),
            run_values_all,
            preferred_element_type=jnp.float32,
        )
        run_attended = run_attended.reshape(run_row_count, width).astype(jnp.bfloat16)
        run_middle = (
            run_flat_in
            + jnp.dot(run_attended, run_w_out, preferred_element_type=jnp.float32)
            + run_b_out.astype(jnp.float32)
        )
        run_second = layer_norm(run_middle, run_g_second, run_s_second).astype(jnp.bfloat16)
        run_pre_act = jnp.dot(
            run_second, run_w_fc, preferred_element_type=jnp.float32
        ) + run_b_fc.astype(jnp.float32)
        run_hidden = gelu_tanh(run_pre_act).astype(jnp.bfloat16)
        result = (
            run_middle
            + jnp.dot(run_hidden, run_w_down, preferred_element_type=jnp.float32)
            + run_b_down.astype(jnp.float32)
        )
        run_kept = (
            run_flat_in,
            run_normed,
            run_queries,
            run_keys_all,
            run_values_all,
            run_importance,
            run_threshold,
            run_log_total,
            run_attended,
            run_middle,
            run_second,
            run_pre_act,
            run_hidden,
            run_allowed,
            run_lower,
            run_segment,
        )
        result, kept = (result.astype(jnp.bfloat16).reshape(run_seq_here, blocks, width), run_kept)
        results.append(result)
        kept_all.append(kept)
        held.append(whole)
    input_grads = [None] * MB
    totals = None
    for batch in reversed(range(MB)):
        bounds = doc_bounds[batch * per_batch : (batch + 1) * per_batch]
        grad_out = cotangent[batch * per_batch : (batch + 1) * per_batch]
        whole = (
            lax.all_gather(first_gain, "dp", axis=0, tiled=True),
            lax.all_gather(first_shift, "dp", axis=0, tiled=True),
            lax.all_gather(qkv_weight, "dp", axis=0, tiled=True),
            lax.all_gather(qv_bias, "dp", axis=0, tiled=True),
            lax.all_gather(score_weight, "dp", axis=0, tiled=True),
            lax.all_gather(out_weight, "dp", axis=0, tiled=True),
            lax.all_gather(out_bias, "dp", axis=0, tiled=True),
            lax.all_gather(second_gain, "dp", axis=0, tiled=True),
            lax.all_gather(second_shift, "dp", axis=0, tiled=True),
            lax.all_gather(fc_weight, "dp", axis=0, tiled=True),
            lax.all_gather(fc_bias, "dp", axis=0, tiled=True),
            lax.all_gather(down_weight, "dp", axis=0, tiled=True),
            lax.all_gather(down_bias, "dp", axis=0, tiled=True),
        )
        d_input, grads = run_backward(whole, kept_all[batch], bounds, grad_out)
        input_grads[batch] = d_input
        totals = (
            grads
            if totals is None
            else tuple((total_a + total_b for total_a, total_b in zip(totals, grads)))
        )
    totals = (
        lax.psum_scatter(
            totals[0].astype(jnp.bfloat16), "dp", scatter_dimension=0, tiled=True
        ).astype(jnp.float32),
        lax.psum_scatter(
            totals[1].astype(jnp.bfloat16), "dp", scatter_dimension=0, tiled=True
        ).astype(jnp.float32),
        lax.psum_scatter(
            totals[2].astype(jnp.bfloat16), "dp", scatter_dimension=0, tiled=True
        ).astype(jnp.float32),
        lax.psum_scatter(
            totals[3].astype(jnp.bfloat16), "dp", scatter_dimension=0, tiled=True
        ).astype(jnp.float32),
        lax.psum_scatter(
            totals[4].astype(jnp.bfloat16), "dp", scatter_dimension=0, tiled=True
        ).astype(jnp.float32),
        lax.psum_scatter(
            totals[5].astype(jnp.bfloat16), "dp", scatter_dimension=0, tiled=True
        ).astype(jnp.float32),
        lax.psum_scatter(
            totals[6].astype(jnp.bfloat16), "dp", scatter_dimension=0, tiled=True
        ).astype(jnp.float32),
        lax.psum_scatter(
            totals[7].astype(jnp.bfloat16), "dp", scatter_dimension=0, tiled=True
        ).astype(jnp.float32),
        lax.psum_scatter(
            totals[8].astype(jnp.bfloat16), "dp", scatter_dimension=0, tiled=True
        ).astype(jnp.float32),
        lax.psum_scatter(
            totals[9].astype(jnp.bfloat16), "dp", scatter_dimension=0, tiled=True
        ).astype(jnp.float32),
        lax.psum_scatter(
            totals[10].astype(jnp.bfloat16), "dp", scatter_dimension=0, tiled=True
        ).astype(jnp.float32),
        lax.psum_scatter(
            totals[11].astype(jnp.bfloat16), "dp", scatter_dimension=0, tiled=True
        ).astype(jnp.float32),
        lax.psum_scatter(
            totals[12].astype(jnp.bfloat16), "dp", scatter_dimension=0, tiled=True
        ).astype(jnp.float32),
    )
    final = (
        lax.psum(totals[0].astype(jnp.bfloat16), "seq").astype(jnp.float32),
        lax.psum(totals[1].astype(jnp.bfloat16), "seq").astype(jnp.float32),
        lax.psum(totals[2].astype(jnp.bfloat16), "seq").astype(jnp.float32),
        lax.psum(totals[3].astype(jnp.bfloat16), "seq").astype(jnp.float32),
        lax.psum(totals[4].astype(jnp.bfloat16), "seq").astype(jnp.float32),
        lax.psum(totals[5].astype(jnp.bfloat16), "seq").astype(jnp.float32),
        lax.psum(totals[6].astype(jnp.bfloat16), "seq").astype(jnp.float32),
        lax.psum(totals[7].astype(jnp.bfloat16), "seq").astype(jnp.float32),
        lax.psum(totals[8].astype(jnp.bfloat16), "seq").astype(jnp.float32),
        lax.psum(totals[9].astype(jnp.bfloat16), "seq").astype(jnp.float32),
        lax.psum(totals[10].astype(jnp.bfloat16), "seq").astype(jnp.float32),
        lax.psum(totals[11].astype(jnp.bfloat16), "seq").astype(jnp.float32),
        lax.psum(totals[12].astype(jnp.bfloat16), "seq").astype(jnp.float32),
    )
    return (jnp.concatenate(results, axis=0), jnp.concatenate(input_grads, axis=0)) + tuple(final)


def solution(mesh):
    in_specs = (
        P("dp", "seq", None),
        P("dp", None),
        P("dp"),
        P("dp"),
        P("dp", None),
        P("dp"),
        P("dp", None),
        P("dp", None),
        P("dp"),
        P("dp"),
        P("dp"),
        P("dp", None),
        P("dp"),
        P("dp", None),
        P("dp"),
        P("dp", "seq", None),
    )
    out_specs = (
        P("dp", "seq", None),
        P("dp", "seq", None),
        P("dp"),
        P("dp"),
        P("dp", None),
        P("dp"),
        P("dp", None),
        P("dp", None),
        P("dp"),
        P("dp"),
        P("dp"),
        P("dp", None),
        P("dp"),
        P("dp", None),
        P("dp"),
    )
    return jax.shard_map(body, mesh=mesh, in_specs=in_specs, out_specs=out_specs, check_vma=False)
```

profile of v0, /device:TPU:0, one launch (start us, length us, event | category | flops | bytes accessed | tf_op | source)
XLA Modules:
  0.0 694.4 jit_solution(15097916141905976293)
XLA Ops:
  18.5 17.7 %all-reduce.28 = (bf16[768]{0:T(1024)(128)(2,1)S(1)}, bf16[768]{0:T(1024)(128)(2,1)S(1)}, bf16[768]{0:T(1024)(128)(2,1)S(1)}, bf16[768]{0:T(1024)(128)(2,1)S(1)}, bf16[768]{0:T(1024)(128)(2,1)S(1)}) all-reduce(bf16[768]{0:T(1024)(128)(2,1)S(1)} %dynamic-update-slice.3, ...), channel_id=1, replica_groups=mesh['seq'=8,'dp'=4] {'dp'}, use_global_device_ids=true, to_apply=%add.9 | all-reduce | flops 3840 | bytes 15360
  36.8 13.6 %all-reduce.24 = (f32[32]{0:T(128)S(1)}, f32[32]{0:T(128)S(1)}, f32[32]{0:T(128)S(1)}, f32[32]{0:T(128)S(1)}) all-reduce(f32[32]{0:T(128)S(1)} %bitcast_dynamic-update-slice_fusion.8, f32[32]{0:T(128)S(1)} %bitcast_dynamic-update-slice_fusion.9, f32[32]{0:T(128)S(1)} %bitcast_dynamic-update-slice_fusion.6, ...), channel_id=9, replica_groups=mesh['seq'=8,'dp'=4] {'seq'}, use_global_device_ids=true, to_apply=%add.13 | all-reduce | flops 128 | bytes 1024
  51.3 7.4 %all-gather.10 = bf16[4,1,384]{2,1,0:T(2,128)(2,1)S(1)} all-gather(bf16[1,1,384]{2,1,0:T(2,128)(2,1)S(1)} %reshape.1535), channel_id=1, replica_groups=mesh['seq'=8,'dp'=4] {'dp'}, dimensions={0}, use_global_device_ids=true | all-gather | bytes 3840 | tf_op jit(solution)/shard_map/all_gather | solution.py:286
  58.7 7.9 %all-gather.14 = bf16[4,1,768]{2,1,0:T(2,128)(2,1)S(1)} all-gather(bf16[1,1,768]{2,1,0:T(2,128)(2,1)S(1)} %reshape.1543), channel_id=1, replica_groups=mesh['seq'=8,'dp'=4] {'dp'}, dimensions={0}, use_global_device_ids=true | all-gather | bytes 7680 | tf_op jit(solution)/shard_map/all_gather | solution.py:293
  67.4 7.6 %all-gather.11 = bf16[4,192,12]{1,2,0:T(8,128)(2,1)S(1)} all-gather(bf16[1,192,12]{1,2,0:T(8,128)(2,1)S(1)} %bitcast.416), channel_id=1, replica_groups=mesh['seq'=8,'dp'=4] {'dp'}, dimensions={0}, use_global_device_ids=true | all-gather | bytes 23040 | tf_op jit(solution)/shard_map/all_gather | solution.py:287
  77.8 12.7 %all-gather.13 = f32[8,4,12]{2,1,0:T(4,128)S(1)} all-gather(f32[1,4,12]{2,1,0:T(4,128)S(1)} %bitcast.417), channel_id=8, replica_groups=mesh['seq'=8,'dp'=4] {'seq'}, dimensions={0}, use_global_device_ids=true | all-gather | bytes 1728 | tf_op jit(solution)/shard_map/all_gather | solution.py:21
  90.7 12.7 %all-gather.16 = f32[8,4,12]{2,1,0:T(4,128)S(1)} all-gather(f32[1,4,12]{2,1,0:T(4,128)S(1)} %bitcast.418), channel_id=11, replica_groups=mesh['seq'=8,'dp'=4] {'seq'}, dimensions={0}, use_global_device_ids=true | all-gather | bytes 1728 | tf_op jit(solution)/shard_map/all_gather | solution.py:21
  103.4 12.7 %all-gather.12 = f32[8,4,12]{2,1,0:T(4,128)S(1)} all-gather(f32[1,4,12]{2,1,0:T(4,128)S(1)} %bitcast.408), channel_id=7, replica_groups=mesh['seq'=8,'dp'=4] {'seq'}, dimensions={0}, use_global_device_ids=true | all-gather | bytes 1728 | tf_op jit(solution)/shard_map/all_gather | solution.py:21
  116.6 13.0 %all-gather.15 = f32[8,4,12]{2,1,0:T(4,128)S(1)} all-gather(f32[1,4,12]{2,1,0:T(4,128)S(1)} %bitcast.409), channel_id=10, replica_groups=mesh['seq'=8,'dp'=4] {'seq'}, dimensions={0}, use_global_device_ids=true | all-gather | bytes 1728 | tf_op jit(solution)/shard_map/all_gather | solution.py:21
  207.6 8.2 %fusion.208 = f32[512,3072]{1,0:T(8,128)} fusion(bf16[768,3072]{1,0:T(8,128)(2,1)} %all-gather.28.cloned.1.call-done, f32[512,768]{1,0:T(8,128)} %copy-done.38, f32[768]{0:T(1024)S(1)} %copy-done.98, f32[768]{0:T(1024)S(1)} %convert_element_type.528, f32[512]{0:T(512)S(1)} %fusion.178, f32[512]{0:T(512)S(1)} %broadcast_multiply_fusion.1), kind=kOutput, calls=%fused_computation.409 | convolution fusion | flops 2417885184 | bytes 12593152 | tf_op jit(solution)/shard_map/dot_general | solution.py:391
  215.7 9.8 %convert_reduce_fusion = (f32[3072]{0:T(1024)S(1)}, bf16[512,3072]{1,0:T(8,128)(2,1)S(1)}) fusion(f32[512,3072]{1,0:T(8,128)} %fusion.208, f32[3072]{0:T(1024)S(1)} %bitcast.410, bf16[512,768]{1,0:T(8,128)(2,1)} %bitcast.380, bf16[3072,768]{1,0:T(8,128)(2,1)} %all-gather.30.cloned.1.call-done), kind=kOutput, calls=%fused_computation.63 | convolution fusion | flops 2452091904 | bytes 14966784 | tf_op jit(solution)/shard_map/nd,fd->nf/dot_general | solution.py:161
  268.8 6.8 convert_reduce_fusion.1
  288.4 6.0 fusion.75
  317.0 18.0 %all-gather.17 = f32[8,4,12]{2,1,0:T(4,128)S(1)} all-gather(f32[1,4,12]{2,1,0:T(4,128)S(1)} %bitcast.419), channel_id=13, replica_groups=mesh['seq'=8,'dp'=4] {'seq'}, dimensions={0}, use_global_device_ids=true | all-gather | bytes 1728 | tf_op jit(solution)/shard_map/all_gather | solution.py:21
  347.4 15.3 %all-gather.18 = f32[8,4,12]{2,1,0:T(4,128)S(1)} all-gather(f32[1,4,12]{2,1,0:T(4,128)S(1)} %bitcast.420), channel_id=15, replica_groups=mesh['seq'=8,'dp'=4] {'seq'}, dimensions={0}, use_global_device_ids=true | all-gather | bytes 1728 | tf_op jit(solution)/shard_map/all_gather | solution.py:21
  397.5 9.0 %add_convert_fusion = bf16[3072,768]{1,0:T(8,128)(2,1)} fusion(f32[3072,768]{1,0:T(8,128)S(1)} %fusion.215, bf16[512,768]{1,0:T(8,128)(2,1)S(1)} %bitcast.381, f32[512,3072]{1,0:T(8,128)} %fusion.208, f32[3072]{0:T(1024)S(1)} %bitcast.413), kind=kOutput, calls=%fused_computation.34 | convolution fusion | flops 2436366336 | bytes 21245952 | tf_op jit(solution)/shard_map/nf,nd->fd/dot_general | solution.py:159
  436.3 16.4 %all-reduce.27 = (bf16[768]{0:T(1024)(128)(2,1)S(1)}, bf16[768]{0:T(1024)(128)(2,1)S(1)}, bf16[768]{0:T(1024)(128)(2,1)S(1)}, bf16[1536]{0:T(1024)(128)(2,1)S(1)...) all-reduce(bf16[768]{0:T(1024)(128)(2,1)S(1)} %dynamic-update-slice, ...), channel_id=1, replica_groups=mesh['seq'=8,'dp'=4] {'dp'}, use_global_device_ids=true, to_apply=%add.12 | all-reduce | flops 9984 | bytes 39936
  452.8 9.5 %add_convert_fusion.4 = bf16[512,768]{1,0:T(8,128)(2,1)} fusion(f32[512,768]{1,0:T(8,128)} %copy-done.41, bf16[3072,768]{1,0:T(8,128)(2,1)} %all-gather.30.cloned.1.call-done, f32[768]{0:T(1024)S(1)} %convert_element_type.533, f32[512,3072]{1,0:T(8,128)} %copy-done.122, f32[3072]{0:T(1024)S(1)} %bitcast.414), kind=kOutput, calls=%fused_computation.198 | convolution fusion | flops 2432827392 | bytes 13384704 | tf_op jit(solution)/shard_map/dot_general | solution.py:397
  462.2 8.8 %reduce-scatter.8.cloned.1.call-done = bf16[192,2304]{1,0:T(8,128)(2,1)} async-done(((bf16[768,2304]{1,0:T(8,128)(2,1)}), bf16[192,2304]{1,0:T(8,128)(2,1)}) %reduce-scatter.8.cloned.1.call-update) | async-done | bytes 884752 | tf_op jit(solution)/shard_map/reduce_scatter | solution.py:456
  471.1 60.1 %reduce-scatter.14.cloned.1.call-done = bf16[768,768]{1,0:T(8,128)(2,1)} async-done(((bf16[3072,768]{1,0:T(8,128)(2,1)}), bf16[768,768]{1,0:T(8,128)(2,1)}) %reduce-scatter.14.cloned.1.call-update) | async-done | bytes 1179664 | tf_op jit(solution)/shard_map/reduce_scatter | solution.py:483
  531.2 60.1 %reduce-scatter.12.cloned.1.call-done = bf16[192,3072]{1,0:T(8,128)(2,1)} async-done(((bf16[768,3072]{1,0:T(8,128)(2,1)}), bf16[192,3072]{1,0:T(8,128)(2,1)}) %reduce-scatter.12.cloned.1.call-update) | async-done | bytes 1179664 | tf_op jit(solution)/shard_map/reduce_scatter | solution.py:477
  591.3 9.5 %add_convert_fusion.6 = bf16[512,768]{1,0:T(8,128)(2,1)} fusion(f32[512,768]{1,0:T(8,128)} %copy-done.38, bf16[3072,768]{1,0:T(8,128)(2,1)} %all-gather.30.cloned.1.call-done, f32[768]{0:T(1024)S(1)} %convert_element_type.533, f32[512,3072]{1,0:T(8,128)} %fusion.208, f32[3072]{0:T(1024)S(1)} %bitcast.415), kind=kOutput, calls=%fused_computation.201 | convolution fusion | flops 2432827392 | bytes 13384704 | tf_op jit(solution)/shard_map/dot_general | solution.py:397
  601.4 30.6 %all-reduce.25 = (bf16[192]{0:T(256)(128)(2,1)S(1)}, bf16[192]{0:T(256)(128)(2,1)S(1)}, bf16[384]{0:T(512)(128)(2,1)S(1)}, bf16[192,12]{0,1:T(8,128)(2,1)S(1)}, ...) all-reduce(bf16[192]{0:T(256)(128)(2,1)S(1)} %dynamic-slice.11, ...), channel_id=1, replica_groups=mesh['seq'=8,'dp'=4] {'seq'}, use_global_device_ids=true, to_apply=%region_43.44 | all-reduce | flops 4608 | bytes 18432 | tf_op jit(solution)/shard_map/psum | solution.py:491
  644.6 35.1 %all-reduce.31.cloned.1.call-done = (bf16[192,2304]{1,0:T(8,128)(2,1)}, bf16[192,768]{1,0:T(8,128)(2,1)}, bf16[192,3072]{1,0:T(8,128)(2,1)}, bf16[768,768]{1,0:T(8,128)(2,1)}) async-done(((bf16[192,2304]{1,0:T(8,128)(2,1)}, bf16[192,768]{1,0:T(8,128)(2,1)}, bf16[192,3072]{1,0:T(8,128)(2,1)}, bf16[768,768]{1,0:T(8,128)(2,1)}), (bf16[192,2304]{1,0:T(8,128)(2,1)}, bf16[192,768]{1,0:T(8,128)(2,1)}, ...) | async-done | bytes 3538960 | tf_op jit(solution)/shard_map/psum | solution.py:493
  (607 shorter events, 266.7 us)
Async XLA Ops:
  7.2 136.0 %all-gather.24.cloned.1.call-start = ((), (), s32[]{:S(2)}) async-start(), calls=%async_computation.5 | async-start | bytes 4423680 | tf_op jit(solution)/shard_map/all_gather | solution.py:285
  7.9 195.4 %all-gather.26.cloned.1.call-start = ((), (), s32[]{:S(2)}) async-start(), calls=%async_computation.6 | async-start | bytes 1474560 | tf_op jit(solution)/shard_map/all_gather | solution.py:288
  8.7 198.9 %all-gather.28.cloned.1.call-start = ((), (), s32[]{:S(2)}) async-start(), calls=%async_computation.7 | async-start | bytes 5898240 | tf_op jit(solution)/shard_map/all_gather | solution.py:292
  9.5 206.2 %all-gather.30.cloned.1.call-start = ((), (), s32[]{:S(2)}) async-start(), calls=%async_computation.8 | async-start | bytes 5898240 | tf_op jit(solution)/shard_map/all_gather | solution.py:294
  10.1 410.8 %reduce-scatter.16.cloned.1.call-start = ((), (), s32[]{:S(2)}) async-start(), calls=%async_computation.13 | async-start | bytes 245760
  11.5 64.2 %copy-start.83 = (f32[4,128]{1,0:T(4,128)}, f32[4,128]{1,0:T(4,128)S(1)}, u32[]{:S(2)}) copy-start(f32[4,128]{1,0:T(4,128)S(1)} %get-tuple-element.697) | copy-start | bytes 6148
  11.5 64.2 %copy-start.85 = (f32[4,128]{1,0:T(4,128)}, f32[4,128]{1,0:T(4,128)S(1)}, u32[]{:S(2)}) copy-start(f32[4,128]{1,0:T(4,128)S(1)} %get-tuple-element.748) | copy-start | bytes 6148
  11.5 126.9 %copy-start.52 = (f32[512]{0:T(512)}, f32[512]{0:T(512)S(1)}, u32[]{:S(2)}) copy-start(f32[512]{0:T(512)S(1)} %get-tuple-element.696) | copy-start | bytes 6148
  11.6 126.9 %copy-start.54 = (f32[512]{0:T(512)}, f32[512]{0:T(512)S(1)}, u32[]{:S(2)}) copy-start(f32[512]{0:T(512)S(1)} %get-tuple-element.749) | copy-start | bytes 6148
  12.7 63.6 %copy-start.107 = (f32[4,128]{1,0:T(4,128)}, f32[4,128]{1,0:T(4,128)S(1)}, u32[]{:S(2)}) copy-start(f32[4,128]{1,0:T(4,128)S(1)} %fusion.180) | copy-start | bytes 6148
  13.3 120.5 %copy-start.76 = (pred[128,128]{1,0:T(8,128)(4,1)}, pred[128,128]{1,0:T(8,128)(4,1)S(1)}, u32[]{:S(2)}) copy-start(pred[128,128]{1,0:T(8,128)(4,1)S(1)} %iota_compare_fusion) | copy-start | bytes 49156
  163.1 35.1 %collective-permute-start = (bf16[4,64,12,64]{1,3,2,0:T(8,128)(2,1)}, bf16[4,64,12,64]{1,3,2,0:T(8,128)(2,1)}, u32[]{:S(2)}, u32[]{:S(2)}) collective-permute-start(bf16[4,64,12,64]{1,3,2,0:T(8,128)(2,1)} %slice.219), channel_id=1, source_target_pairs={{0,4},{4,8},{8,12},{12,16},{16,20},{20,24},{24,28},{1,5},{5,9},{9,... | collective-permute-start | bytes 1179656 | tf_op jit(solution)/shard_map/ppermute | solution.py:39
  166.2 26.4 %collective-permute-start.1 = (bf16[4,64,12,64]{1,3,2,0:T(8,128)(2,1)}, bf16[4,64,12,64]{1,3,2,0:T(8,128)(2,1)}, u32[]{:S(2)}, u32[]{:S(2)}) collective-permute-start(bf16[4,64,12,64]{1,3,2,0:T(8,128)(2,1)} %slice.222), channel_id=1, source_target_pairs={{0,4},{4,8},{8,12},{12,16},{16,20},{20,24},{24,28},{1,5},{5,9},{9,... | collective-permute-start | bytes 1179656 | tf_op jit(solution)/shard_map/ppermute | solution.py:39
  187.7 65.5 %collective-permute-start.3 = (bf16[4,64,12,64]{1,3,2,0:T(8,128)(2,1)}, bf16[4,64,12,64]{1,3,2,0:T(8,128)(2,1)}, u32[]{:S(2)}, u32[]{:S(2)}) collective-permute-start(bf16[4,64,12,64]{1,3,2,0:T(8,128)(2,1)} %slice.228), channel_id=1, source_target_pairs={{0,4},{4,8},{8,12},{12,16},{16,20},{20,24},{24,28},{1,5},{5,9},{9,... | collective-permute-start | bytes 1179656 | tf_op jit(solution)/shard_map/ppermute | solution.py:39
  189.9 71.4 %collective-permute-start.2 = (bf16[4,64,12,64]{1,3,2,0:T(8,128)(2,1)}, bf16[4,64,12,64]{1,3,2,0:T(8,128)(2,1)}, u32[]{:S(2)}, u32[]{:S(2)}) collective-permute-start(bf16[4,64,12,64]{1,3,2,0:T(8,128)(2,1)} %slice.225), channel_id=1, source_target_pairs={{0,4},{4,8},{8,12},{12,16},{16,20},{20,24},{24,28},{1,5},{5,9},{9,... | collective-permute-start | bytes 1179656 | tf_op jit(solution)/shard_map/ppermute | solution.py:39
  307.0 63.2 %collective-permute-start.5 = (bf16[4,64,12,64]{1,3,2,0:T(8,128)(2,1)}, bf16[4,64,12,64]{1,3,2,0:T(8,128)(2,1)}, u32[]{:S(2)}, u32[]{:S(2)}) collective-permute-start(bf16[4,64,12,64]{1,3,2,0:T(8,128)(2,1)} %slice.322), channel_id=1, source_target_pairs={{4,0},{8,4},{12,8},{16,12},{20,16},{24,20},{28,24},{5,1},{9,5},{13... | collective-permute-start | bytes 1179656 | tf_op jit(solution)/shard_map/ppermute | solution.py:39
  314.6 58.5 %collective-permute-start.4 = (bf16[4,64,12,64]{1,3,2,0:T(8,128)(2,1)}, bf16[4,64,12,64]{1,3,2,0:T(8,128)(2,1)}, u32[]{:S(2)}, u32[]{:S(2)}) collective-permute-start(bf16[4,64,12,64]{1,3,2,0:T(8,128)(2,1)} %slice.323), channel_id=1, source_target_pairs={{4,0},{8,4},{12,8},{16,12},{20,16},{24,20},{28,24},{5,1},{9,5},{13... | collective-permute-start | bytes 1179656 | tf_op jit(solution)/shard_map/ppermute | solution.py:39
  341.7 33.6 %collective-permute-start.7 = (bf16[4,64,12,64]{1,3,2,0:T(8,128)(2,1)}, bf16[4,64,12,64]{1,3,2,0:T(8,128)(2,1)}, u32[]{:S(2)}, u32[]{:S(2)}) collective-permute-start(bf16[4,64,12,64]{1,3,2,0:T(8,128)(2,1)} %slice.320), channel_id=1, source_target_pairs={{4,0},{8,4},{12,8},{16,12},{20,16},{24,20},{28,24},{5,1},{9,5},{13... | collective-permute-start | bytes 1179656 | tf_op jit(solution)/shard_map/ppermute | solution.py:39
  366.0 96.2 %reduce-scatter.10.cloned.1.call-start = ((), (), s32[]{:S(2)}) async-start(), calls=%async_computation.10 | async-start | bytes 1474560 | tf_op jit(solution)/shard_map/reduce_scatter | solution.py:465
  367.6 9.7 %collective-permute-start.6 = (bf16[4,64,12,64]{1,3,2,0:T(8,128)(2,1)S(1)}, bf16[4,64,12,64]{1,3,2,0:T(8,128)(2,1)}, u32[]{:S(2)}, u32[]{:S(2)}) collective-permute-start(bf16[4,64,12,64]{1,3,2,0:T(8,128)(2,1)S(1)} %slice.321), channel_id=1, source_target_pairs={{4,0},{8,4},{12,8},{16,12},{20,16},{24,20},{28,24},{5,1},{9,5},{13... | collective-permute-start | bytes 1179656 | tf_op jit(solution)/shard_map/ppermute | solution.py:39
  369.9 101.2 %reduce-scatter.8.cloned.1.call-start = ((), (), s32[]{:S(2)}) async-start(), calls=%async_computation.9 | async-start | bytes 4423680 | tf_op jit(solution)/shard_map/reduce_scatter | solution.py:456
  390.4 140.8 %reduce-scatter.14.cloned.1.call-start = ((), (), s32[]{:S(2)}) async-start(), calls=%async_computation.12 | async-start | bytes 5898240 | tf_op jit(solution)/shard_map/reduce_scatter | solution.py:483
  406.5 184.8 %reduce-scatter.12.cloned.1.call-start = ((), (), s32[]{:S(2)}) async-start(), calls=%async_computation.11 | async-start | bytes 5898240 | tf_op jit(solution)/shard_map/reduce_scatter | solution.py:477
  417.4 262.3 %all-reduce.31.cloned.1.call-start = ((), (), s32[]{:S(2)}) async-start(), calls=%async_computation.14 | async-start | bytes 7077888 | tf_op jit(solution)/shard_map/psum | solution.py:493
  (132 other events, 1165.7 us)
Sparse Core Ops, SparseCore 0:
  9.9 50.1 all-gather.23
  61.9 27.8 all-gather.25
  91.6 57.0 all-gather.27
  150.4 57.0 all-gather.29
  366.1 21.7 reduce-scatter.15
  391.3 28.4 reduce-scatter.9
  422.9 48.1 reduce-scatter.7
  474.1 57.0 reduce-scatter.13
  534.2 57.0 reduce-scatter.11
  593.8 85.8 all-reduce.30
where the time goes:
time: 701 us; the launch traced here: 694 us
  blocking collectives  186 us (27%)
  waiting for transfers between devices  167 us (24%)
  matrix products  161 us (23%)
  local copies, waits for them, and re-layouts  77.7 us (11%)
  other arithmetic  65.8 us (9%)
  between operations  20 us (3%)
  starting transfers between devices  16.7 us (2%)
    all_gather x6, blocking collectives, prefix(): pieces = jax.tree.map(lambda part: lax.all_gather(part, axis), value)  84.5 us
    reduce_scatter x1, waiting for transfers between devices, body(): lax.psum_scatter(totals[9].astype(jnp.bfloat16), 'dp', scatter_dimension=...  60.1 us
    reduce_scatter x1, waiting for transfers between devices, body(): lax.psum_scatter(totals[11].astype(jnp.bfloat16), 'dp', scatter_dimension...  60.1 us
    unnamed x3, blocking collectives  47.7 us
    psum x1, waiting for transfers between devices, body(): lax.psum(totals[2].astype(jnp.bfloat16), 'seq').astype(jnp.float32)  35.1 us
    psum x1, blocking collectives, body(): lax.psum(totals[0].astype(jnp.bfloat16), 'seq').astype(jnp.float32)  30.6 us
    unnamed x321, local copies, waits for them, and re-layouts  21.3 us
    dot_general x2, matrix products, body(): jnp.dot(run_hidden, run_w_down, preferred_element_type=jnp.float32)  18.9 us
  transfers between devices with their start and end apart: 18, of which 4 were waited for; matrix products, arithmetic and copies ran while one was open for 34% of the time, Pallas kernels for 0%

commit v1 on v0

v1 whole, which is shorter than its diff:
```python
import math

import jax
import jax.numpy as jnp
from jax import lax
from jax.experimental import pallas as pl
from jax.experimental.pallas import tpu as pltpu
from jax.sharding import PartitionSpec as P

KTOP = 64
WINDOW = 64
HEAD = 64
LANES = 128
EPSILON = 1e-05
NEGATIVE = -1e30
SCALE = 1.0 / math.sqrt(HEAD)
GELU_A = math.sqrt(2.0 / math.pi)
GELU_B = 0.044715
BF = jnp.bfloat16
F32 = jnp.float32
NN = ((1,), (0,))
NT = ((1,), (1,))
TN = ((0,), (0,))
CHUNKS = 2
BLOCKS = 2
VMEM_LIMIT = 56 * 2**20


def mm(left, right, dims=NN):
    return lax.dot_general(left, right, (dims, ((), ())), preferred_element_type=F32)


def mm_split(mask, value, dims=NN):
    high = value.astype(BF)
    low = (value - high.astype(F32)).astype(BF)
    return mm(mask, high, dims) + mm(mask, low, dims)


def whole_spec(shape):
    return pl.BlockSpec(shape, lambda *_: (0,) * len(shape))


def call(kernel, name, grid, in_specs, out_specs, out_shape, scratch=(), prefetch=0, flops=0, moved=0):
    return pl.pallas_call(
        kernel,
        grid_spec=pltpu.PrefetchScalarGridSpec(
            num_scalar_prefetch=prefetch,
            grid=grid,
            in_specs=in_specs,
            out_specs=out_specs,
            scratch_shapes=list(scratch),
        ),
        out_shape=out_shape,
        compiler_params=pltpu.CompilerParams(vmem_limit_bytes=VMEM_LIMIT),
        cost_estimate=pl.CostEstimate(flops=int(flops), bytes_accessed=int(moved), transcendentals=0),
        name=name,
    )


def iota(shape, axis):
    return lax.broadcasted_iota(jnp.int32, shape, axis)


def segment(places, first, second):
    return (places >= first).astype(jnp.int32) + (places >= second).astype(jnp.int32)


def normalise(values):
    average = jnp.mean(values, axis=-1, keepdims=True)
    centred = values - average
    variance = jnp.mean(centred * centred, axis=-1, keepdims=True)
    scale = lax.rsqrt(variance + EPSILON)
    return centred * scale, scale


def norm_back(d_norm, unit, scale, gain):
    weighted = d_norm * gain
    return scale * (
        weighted
        - jnp.mean(weighted, axis=-1, keepdims=True)
        - unit * jnp.mean(weighted * unit, axis=-1, keepdims=True)
    )


def prep_kernel(info, bounds, x_ref, tail_ref, gain_ref, shift_ref, score_ref, normed_ref, tail_out_ref, imp_ref, mass_ref, stat_ref):
    s = pl.program_id(0)
    blocks = x_ref.shape[0]
    gain = gain_ref[...]
    shift = shift_ref[...]
    normed = (normalise(x_ref[...].astype(F32))[0] * gain + shift).astype(BF)
    normed_ref[...] = normed
    tail_out_ref[...] = (normalise(tail_ref[...].astype(F32))[0] * gain + shift).astype(BF)
    importance = mm(normed, score_ref[...])
    imp_ref[...] = importance
    start = info[0]
    first, second = bounds[2 * s], bounds[2 * s + 1]
    rows = iota((blocks, blocks), 0)
    cols = iota((blocks, blocks), 1)
    lower = (cols <= rows) & (segment(start + rows, first, second) == segment(start + cols, first, second))
    peak = jnp.max(importance, axis=0, keepdims=True)
    mass = mm_split(lower.astype(BF), jnp.exp(importance - peak))
    mass_ref[...] = mass
    stat_ref[0, 0:1, :] = peak
    stat_ref[0, 1:2, :] = mass[blocks - 1 :, :]


def qkv_kernel(normed_ref, tail_ref, weight_ref, bias_ref, out_ref, tail_out_ref):
    j = pl.program_id(0)
    weight = weight_ref[0]
    bias = bias_ref[0]
    factor = jnp.where(j == 0, SCALE, 1.0)
    out_ref[0] = ((mm(normed_ref[...], weight) + bias).astype(BF).astype(F32) * factor).astype(BF)

    @pl.when(j > 0)
    def _():
        tail_out_ref[0] = (mm(tail_ref[...], weight) + bias).astype(BF)


def lane_masks():
    first = (iota((1, LANES), 1) < HEAD)
    return first.astype(BF), (~first).astype(BF)


def grouped(part, keep_first, keep_second):
    return jnp.concatenate([part * keep_first, part * keep_second], axis=0)


def tile_masks(start, half, first, second):
    shape = (WINDOW, LANES)
    row = iota(shape, 0)
    col = iota(shape, 1) & (HEAD - 1)
    base = start + WINDOW * half
    mine = segment(base + row, first, second)
    far = segment(base - WINDOW + col, first, second) == mine
    near = (col <= row) & (segment(base + col, first, second) == mine)
    if half == 0:
        far = far & (col > row) & (base - WINDOW + col >= 0)
    return far, near, col <= row


def spread(columns, pair, rows):
    left = columns[:, 2 * pair : 2 * pair + 1]
    right = columns[:, 2 * pair + 1 : 2 * pair + 2]
    lane = iota((rows, LANES), 1)
    return jnp.where(lane < HEAD, left, right)


def attention_kernel(info, bounds, qkv_ref, halo_ref, imp_ref, mass_ref, peak_ref, before_ref, att_ref, probs_ref, sig_ref, inv_ref):
    s = pl.program_id(0)
    blocks = imp_ref.shape[0]
    start = info[0]
    first, second = bounds[2 * s], bounds[2 * s + 1]
    pairs = att_ref.shape[1] // LANES
    peak = peak_ref[0, 0:1, :]
    carry_peak = before_ref[0, 0:1, :]
    carry_total = before_ref[0, 1:2, :]
    top = before_ref[0, 2:3, :]
    joined = jnp.maximum(peak, carry_peak)
    place = start + iota((blocks, LANES), 0)
    continues = segment(place, first, second) == segment(jnp.full((1, LANES), start - 1, jnp.int32), first, second)
    mass = mass_ref[...] * jnp.exp(peak - joined) + jnp.where(
        continues, carry_total * jnp.exp(carry_peak - joined), 0.0
    )
    threshold = joined + jnp.log(mass) - math.log(KTOP)
    late = threshold[WINDOW:]
    inv_ref[...] = 1.0 / (mass[WINDOW:] * jnp.exp(joined - top))
    imp_rows = imp_ref[...].T
    keep_first, keep_second = lane_masks()
    ones = jnp.ones((WINDOW, LANES), BF)
    one_group = grouped(ones, keep_first, keep_second)
    masks = [tile_masks(start, half, first, second) for half in (0, 1)]
    lane = iota((WINDOW, LANES), 1) < HEAD
    for pair in range(pairs):
        ls = slice(pair * LANES, (pair + 1) * LANES)
        keys = [grouped(part, keep_first, keep_second) for part in (halo_ref[0, :, ls], qkv_ref[1, :WINDOW, ls], qkv_ref[1, WINDOW:, ls])]
        values = [
            jnp.concatenate([grouped(part, keep_first, keep_second), one_group], axis=1)
            for part in (halo_ref[1, :, ls], qkv_ref[2, :WINDOW, ls], qkv_ref[2, WINDOW:, ls])
        ]
        for half in (0, 1):
            rs = slice(half * WINDOW, (half + 1) * WINDOW)
            far_ok, near_ok, gated = masks[half]
            logits = mm(qkv_ref[0, rs, ls], jnp.concatenate(keys[half : half + 2], axis=0), NT)
            far, near = logits[:, :LANES], logits[:, LANES:]
            if half == 1:
                row = jnp.concatenate(
                    [imp_rows[2 * pair : 2 * pair + 1, :WINDOW], imp_rows[2 * pair + 1 : 2 * pair + 2, :WINDOW]], axis=1
                )
                gap = spread(late, pair, WINDOW) - row
                small = jnp.exp(-jnp.abs(gap))
                soft = jnp.maximum(gap, 0.0) + jnp.log(1.0 + small)
                sig_ref[:, ls] = (jnp.where(gap >= 0, 1.0, small) / (1.0 + small)).astype(BF)
                far = jnp.where(gated, far - soft, far)
            far = jnp.where(far_ok, far, NEGATIVE)
            near = jnp.where(near_ok, near, NEGATIVE)
            best = jnp.maximum(far, near)
            best_first = jnp.max(jnp.where(lane, best, NEGATIVE), axis=1, keepdims=True)
            best_second = jnp.max(jnp.where(lane, NEGATIVE, best), axis=1, keepdims=True)
            best = jnp.where(lane, best_first, best_second)
            far = jnp.exp(far - best)
            near = jnp.exp(near - best)
            weights = jnp.concatenate([far.astype(BF), near.astype(BF)], axis=1)
            mixed = mm(weights, jnp.concatenate(values[half : half + 2], axis=0))
            inverse = 1.0 / mixed[:, LANES:]
            att_ref[rs, ls] = (mixed[:, :LANES] * inverse).astype(BF)
            probs_ref[rs, 2 * pair * LANES : (2 * pair + 1) * LANES] = (far * inverse).astype(BF)
            probs_ref[rs, (2 * pair + 1) * LANES : (2 * pair + 2) * LANES] = (near * inverse).astype(BF)


def project_kernel(att_ref, x_ref, weight_ref, bias_ref, gain_ref, shift_ref, middle_ref, second_ref):
    middle = x_ref[...].astype(F32) + mm(att_ref[...], weight_ref[...]) + bias_ref[...]
    middle_ref[...] = middle
    second_ref[...] = (normalise(middle)[0] * gain_ref[...] + shift_ref[...]).astype(BF)


def feed_kernel(*refs, heads_in):
    if heads_in:
        order, sec_ref, dy_ref, fc_ref, down_ref, bias_ref, out_in, dsec_in, out_ref, dsec_ref, keep_ref, send_ref, db_ref = refs
    else:
        order, sec_ref, dy_ref, fc_ref, down_ref, bias_ref, out_ref, dsec_ref, keep_ref, send_ref, db_ref = refs
    j = pl.program_id(0)
    shards = keep_ref.shape[0]
    core = order[0]
    fc = fc_ref[0]
    down = down_ref[0]
    pre = mm(sec_ref[...], fc) + bias_ref[0]
    d_hidden = mm(dy_ref[...], down, NT)
    square = pre * pre
    tanh = jnp.tanh(pre * (GELU_A + GELU_A * GELU_B * square))
    half = 0.5 + 0.5 * tanh
    hidden = (pre * half).astype(BF)
    slope = half + pre * (0.5 * GELU_A + 1.5 * GELU_A * GELU_B * square) * (1.0 - tanh * tanh)
    d_pre = d_hidden * slope
    d_low = d_pre.astype(BF)
    db_ref[0] = jnp.sum(d_pre, axis=0, keepdims=True)
    out = mm(hidden, down)
    d_second = mm(d_low, fc, NT)

    @pl.when(j == 0)
    def _():
        if heads_in:
            out_ref[...] = out_in[...] + out
            dsec_ref[...] = dsec_in[...] + d_second
        else:
            out_ref[...] = out
            dsec_ref[...] = d_second

    @pl.when(j > 0)
    def _():
        out_ref[...] += out
        dsec_ref[...] += d_second

    d_fc = mm(sec_ref[...], d_low, TN).astype(BF)
    d_down = mm(hidden, dy_ref[...], TN).astype(BF)
    rows = d_fc.shape[0] // shards
    per_block = shards // BLOCKS
    deep = d_down.shape[0] // per_block
    where = pl.multiple_of(j * rows, rows)

    def store(fc_to, fc_order, down_to, down_order):
        for shard in range(shards):
            fc_to[order[fc_order + shard], pl.ds(where, rows), :] = d_fc[shard * rows : (shard + 1) * rows]
        for shard in range(per_block):
            down_to[order[down_order + j * per_block + shard]] = d_down[shard * deep : (shard + 1) * deep]

    @pl.when(core == 0)
    def _():
        store(keep_ref, 1, send_ref, 1 + shards)

    @pl.when(core != 0)
    def _():
        store(send_ref, 1 + shards, keep_ref, 1)


def middle_kernel(order, dsec_ref, middle_ref, dy_ref, out_ref, att_ref, weight_ref, gain_ref, down_bias_ref, block_ref, dmid_ref, datt_ref, keep_ref, send_ref, sums_ref, total):
    i = pl.program_id(0)
    steps = pl.num_programs(0)
    shards = keep_ref.shape[0]
    core = order[0]
    middle = middle_ref[...]
    block_ref[...] = (middle + out_ref[...] + down_bias_ref[...]).astype(BF)
    unit, scale = normalise(middle)
    d_norm = dsec_ref[...]
    dy = dy_ref[...].astype(F32)
    d_middle = dy + norm_back(d_norm, unit, scale, gain_ref[...])
    dmid_ref[...] = d_middle
    branch = d_middle.astype(BF)
    datt_ref[...] = mm(branch, weight_ref[...], NT).astype(BF)
    part = mm(att_ref[...], branch, TN)
    sums = [
        jnp.sum(d_norm * unit, axis=0, keepdims=True),
        jnp.sum(d_norm, axis=0, keepdims=True),
        jnp.sum(branch.astype(F32), axis=0, keepdims=True),
        jnp.sum(dy, axis=0, keepdims=True),
    ]

    @pl.when(i == 0)
    def _():
        total[...] = part
        for k in range(4):
            sums_ref[k : k + 1] = sums[k]

    @pl.when(i > 0)
    def _():
        total[...] += part
        for k in range(4):
            sums_ref[k : k + 1] += sums[k]

    @pl.when(i == steps - 1)
    def _():
        rows = total.shape[0] // shards
        half = rows // 2

        def store(side, to, to_order):
            for shard in range(shards):
                begin = shard * rows + side * half
                to[order[to_order + shard]] = total[begin : begin + half].astype(BF)

        @pl.when(core == 0)
        def _():
            store(0, keep_ref, 1)
            store(1, send_ref, 1 + shards)

        @pl.when(core != 0)
        def _():
            store(1, keep_ref, 1)
            store(0, send_ref, 1 + shards)


def attention_back_kernel(info, bounds, qkv_ref, halo_ref, att_ref, datt_ref, probs_ref, sig_ref, inv_ref, imp_ref, before_ref, dqkv_ref, dhalo_ref, dimp_ref, total_ref, rows_scratch):
    s = pl.program_id(0)
    blocks = imp_ref.shape[0]
    start = info[0]
    first, second = bounds[2 * s], bounds[2 * s + 1]
    pairs = att_ref.shape[1] // LANES
    keep_first, keep_second = lane_masks()
    ones = jnp.ones((WINDOW, LANES), BF)
    one_group = grouped(ones, keep_first, keep_second)
    lane = iota((WINDOW, LANES), 1) < HEAD
    gated = (iota((WINDOW, LANES), 1) & (HEAD - 1)) <= iota((WINDOW, LANES), 0)
    head_lane = iota((LANES, LANES), 1)
    head_row = iota((LANES, LANES), 0)
    d_threshold = jnp.zeros((WINDOW, LANES), F32)
    rows_scratch[...] = jnp.zeros_like(rows_scratch)
    for pair in range(pairs):
        ls = slice(pair * LANES, (pair + 1) * LANES)
        keys = [grouped(part, keep_first, keep_second) for part in (halo_ref[0, :, ls], qkv_ref[1, :WINDOW, ls], qkv_ref[1, WINDOW:, ls])]
        values = [
            jnp.concatenate([grouped(part, keep_first, keep_second), one_group], axis=1)
            for part in (halo_ref[1, :, ls], qkv_ref[2, :WINDOW, ls], qkv_ref[2, WINDOW:, ls])
        ]
        far_keys, near_keys, far_values, near_values = [], [], [], []
        for half in (0, 1):
            rs = slice(half * WINDOW, (half + 1) * WINDOW)
            d_out = datt_ref[rs, ls]
            product = (-(d_out.astype(F32) * att_ref[rs, ls].astype(F32))).astype(BF)
            left = jnp.concatenate([d_out, product], axis=1)
            centred = mm(left, jnp.concatenate(values[half : half + 2], axis=0), NT)
            probs = probs_ref[rs, 2 * pair * LANES : (2 * pair + 2) * LANES]
            d_logits = probs.astype(F32) * centred
            low = d_logits.astype(BF)
            dqkv_ref[0, rs, ls] = (mm(low, jnp.concatenate(keys[half : half + 2], axis=0)) * SCALE).astype(BF)
            d_keys = mm(low, qkv_ref[0, rs, ls], TN)
            d_values = mm(probs, d_out, TN)
            far_keys.append(jnp.where(lane, d_keys[:WINDOW], d_keys[WINDOW : 2 * WINDOW]))
            near_keys.append(jnp.where(lane, d_keys[2 * WINDOW : 3 * WINDOW], d_keys[3 * WINDOW :]))
            far_values.append(jnp.where(lane, d_values[:WINDOW], d_values[WINDOW : 2 * WINDOW]))
            near_values.append(jnp.where(lane, d_values[2 * WINDOW : 3 * WINDOW], d_values[3 * WINDOW :]))
            if half == 1:
                gate = jnp.where(gated, d_logits[:, :LANES] * sig_ref[:, ls].astype(F32), 0.0)
                rows_scratch[pair : pair + 1, :] = jnp.sum(gate, axis=0, keepdims=True)
                chosen = (head_lane == 2 * pair + (head_row >= HEAD).astype(jnp.int32)).astype(BF)
                d_threshold = d_threshold - mm(gate.astype(BF), chosen)
        dhalo_ref[0, :, ls] = far_keys[0].astype(BF)
        dhalo_ref[1, :, ls] = far_values[0].astype(BF)
        dqkv_ref[1, :WINDOW, ls] = (near_keys[0] + far_keys[1]).astype(BF)
        dqkv_ref[1, WINDOW:, ls] = near_keys[1].astype(BF)
        dqkv_ref[2, :WINDOW, ls] = (near_values[0] + far_values[1]).astype(BF)
        dqkv_ref[2, WINDOW:, ls] = near_values[1].astype(BF)
    weighted = d_threshold * inv_ref[...]
    row = iota((blocks, WINDOW), 0)
    col = iota((blocks, WINDOW), 1) + WINDOW
    after = (col >= row) & (segment(start + row, first, second) == segment(start + col, first, second))
    later = mm_split(after.astype(BF), weighted)
    total_ref[0, 0:1, :] = later[0:1]
    turned = rows_scratch[...].T
    pick_first = (head_lane == 2 * head_row).astype(BF)
    pick_second = (head_lane == 2 * head_row + 1).astype(BF)

    def pick(values, chosen):
        high = values.astype(BF)
        return mm(high, chosen) + mm((values - high.astype(F32)).astype(BF), chosen)

    direct = pick(turned[:HEAD], pick_first) + pick(turned[HEAD:], pick_second)
    local = jnp.exp(imp_ref[...] - before_ref[0, 2:3, :]) * later
    dimp_ref[:WINDOW] = local[:WINDOW] + direct
    dimp_ref[WINDOW:] = local[WINDOW:]


def tail_back_kernel(dhalo_ref, weight_ref, x_ref, gain_ref, out_ref, sums_ref):
    d_norm = mm(dhalo_ref[0], weight_ref[1], NT) + mm(dhalo_ref[1], weight_ref[2], NT)
    unit, scale = normalise(x_ref[...].astype(F32))
    out_ref[...] = norm_back(d_norm, unit, scale, gain_ref[...]).astype(BF)
    sums_ref[0:1] = jnp.sum(d_norm * unit, axis=0, keepdims=True)
    sums_ref[1:2] = jnp.sum(d_norm, axis=0, keepdims=True)


def qkv_grad_kernel(order, normed_ref, tail_ref, dqkv_ref, dhalo_ref, keep_ref, send_ref, sums_ref):
    j = pl.program_id(0)
    shards = keep_ref.shape[0]
    core = order[0]
    local = dqkv_ref[0]
    halo = jnp.where(j > 0, dhalo_ref[0], jnp.zeros_like(dhalo_ref[0]))
    total = (mm(normed_ref[...], local, TN) + mm(tail_ref[...], halo, TN)).astype(BF)
    sums_ref[0] = jnp.sum(local.astype(F32), axis=0, keepdims=True) + jnp.sum(halo.astype(F32), axis=0, keepdims=True)
    rows = total.shape[0] // shards
    half = rows // 2

    def store(side, to, to_order):
        for shard in range(shards):
            begin = shard * rows + side * half
            to[order[to_order + shard], pl.ds(pl.multiple_of(j * half, half), half), :] = total[begin : begin + half]

    @pl.when(core == 0)
    def _():
        store(0, keep_ref, 1)
        store(1, send_ref, 1 + shards)

    @pl.when(core != 0)
    def _():
        store(1, keep_ref, 1)
        store(0, send_ref, 1 + shards)


def input_grad_kernel(info, bounds, dqkv_ref, weight_ref, score_ref, normed_ref, x_ref, gain_ref, dmid_ref, back_ref, dimp_ref, imp_ref, before_ref, after_ref, out_ref, sums_ref, score_out_ref):
    i = pl.program_id(0)
    seqs = back_ref.shape[0]
    blocks = x_ref.shape[0] // seqs
    start = info[0]
    d_imps = []
    for s in range(seqs):
        first, second = bounds[2 * (i * seqs + s)], bounds[2 * (i * seqs + s) + 1]
        place = start + iota((blocks, LANES), 0)
        onward = segment(place, first, second) == segment(jnp.full((1, LANES), start + blocks, jnp.int32), first, second)
        rs = slice(s * blocks, (s + 1) * blocks)
        extra = jnp.exp(imp_ref[rs] - before_ref[s, 2:3, :]) * after_ref[s, 0:1, :]
        d_imps.append(dimp_ref[rs] + jnp.where(onward, extra, 0.0))
    d_imp = jnp.concatenate(d_imps, axis=0).astype(BF)
    d_norm = mm(d_imp, score_ref[...], NT)
    for j in range(3):
        d_norm = d_norm + mm(dqkv_ref[j], weight_ref[j], NT)
    unit, scale = normalise(x_ref[...].astype(F32))
    d_value = norm_back(d_norm, unit, scale, gain_ref[...]) + dmid_ref[...]
    for s in range(seqs):
        rs = slice(s * blocks, s * blocks + WINDOW)
        out_ref[rs] = d_value[rs]
        rs = slice(s * blocks + WINDOW, (s + 1) * blocks)
        out_ref[rs] = d_value[rs] + back_ref[s].astype(F32)
    sums = [jnp.sum(d_norm * unit, axis=0, keepdims=True), jnp.sum(d_norm, axis=0, keepdims=True)]
    score = mm(normed_ref[...], d_imp, TN)

    @pl.when(i == 0)
    def _():
        score_out_ref[...] = score
        for k in range(2):
            sums_ref[k : k + 1] = sums[k]

    @pl.when(i > 0)
    def _():
        score_out_ref[...] += score
        for k in range(2):
            sums_ref[k : k + 1] += sums[k]


class Net:
    def __init__(self):
        self.n_seq = lax.axis_size("seq")
        self.n_dp = lax.axis_size("dp")
        self.seq = lax.axis_index("seq")
        self.dp = lax.axis_index("dp")
        self.core = self.seq % 2
        self.bits = self.n_dp.bit_length() - 1
        half = self.bits // 2
        straight = list(range(self.bits))
        self.orders = (straight, straight[half:] + straight[:half])

    def send(self, value, target):
        pairs = []
        for s in range(self.n_seq):
            for d in range(self.n_dp):
                goal = target(s, d)
                if goal is not None and 0 <= goal[0] < self.n_seq:
                    pairs.append((s * self.n_dp + d, goal[0] * self.n_dp + goal[1]))
        return lax.ppermute(value, ("seq", "dp"), pairs)

    def across(self, value, step):
        return self.send(value, lambda s, d: (s, d ^ (1 << self.orders[s % 2][step])))

    def chip(self, value):
        return self.send(value, lambda s, d: (s ^ 1, d))

    def along(self, value, bit):
        return self.send(value, lambda s, d: (s ^ (1 << bit), d))

    def shifted(self, value, by):
        return self.send(value, lambda s, d: (s + by, d))

    def table(self, order, first_high):
        far = jnp.arange(self.n_dp, dtype=jnp.int32) ^ self.dp
        index = jnp.zeros_like(far)
        for step, bit in enumerate(order):
            place = self.bits - 1 - step if first_high else step
            index = index | (((far >> bit) & 1) << place)
        return index

    def tables(self, first_high):
        even, odd = (self.table(order, first_high) for order in self.orders)
        mine = jnp.where(self.core == 0, even, odd)
        other = jnp.where(self.core == 0, odd, even)
        return mine, other

    def gather(self, own):
        held = own[None]
        for step in range(self.bits):
            held = jnp.concatenate([held, self.across(held, step)], axis=0)
        return held

    def reduce(self, current):
        size = self.n_dp
        for step in range(self.bits):
            size //= 2
            got = self.across(current[size:], step)
            current = add(current[:size], got)
        current = current[0]
        z_bits = (self.n_seq // 2).bit_length() - 1
        half = current.shape[0] // 2
        upper = (self.seq // 2) % 2
        low, high = current[:half], current[half:]
        kept = jnp.where(upper == 1, high, low)
        given = jnp.where(upper == 1, low, high)
        kept = add(kept, self.along(given, 1))
        for bit in range(1, z_bits):
            kept = add(kept, self.along(kept, bit + 1))
        got = self.along(kept, 1)
        low = jnp.where(upper == 1, got, kept)
        high = jnp.where(upper == 1, kept, got)
        return jnp.concatenate([low, high], axis=0)

    def sum_all(self, value):
        value = value + self.chip(value)
        for step in range(self.bits):
            value = value + self.across(value, step)
        for bit in range(1, self.n_seq.bit_length() - 1):
            value = value + self.along(value, bit)
        return value


def add(left, right):
    return (left.astype(F32) + right.astype(F32)).astype(BF)


def combine(peak_a, total_a, peak_b, total_b):
    joined = jnp.maximum(peak_a, peak_b)
    return joined, total_a * jnp.exp(peak_a - joined) + total_b * jnp.exp(peak_b - joined)


def body(block_input, doc_bounds, first_gain, first_shift, qkv_weight, qv_bias, score_weight, out_weight, out_bias, second_gain, second_shift, fc_weight, fc_bias, down_weight, down_bias, cotangent):
    net = Net()
    seqs, blocks, width = block_input.shape
    tokens = seqs * blocks
    heads = score_weight.shape[1]
    shards = net.n_dp
    rows = width // shards
    hidden = fc_weight.shape[1]
    tail = seqs * WINDOW
    start = (net.seq * blocks).astype(jnp.int32)
    info = jnp.reshape(start, (1,))
    bounds = doc_bounds.reshape(-1)
    x_flat = block_input.reshape(tokens, width)
    dy = cotangent.reshape(tokens, width)
    core = net.core.astype(jnp.int32)

    small_parts = [first_gain, first_shift, second_gain, second_shift, out_bias, down_bias, qv_bias, fc_bias, score_weight.reshape(-1)]
    sizes = [part.shape[0] for part in small_parts]
    packed = jnp.concatenate(small_parts)
    got_small = net.gather(packed.reshape(-1, LANES) if packed.shape[0] % LANES == 0 else packed.reshape(1, -1))
    mine_gather, other_gather = net.tables(False)
    mine_reduce, other_reduce = net.tables(True)
    order = jnp.concatenate([jnp.reshape(core, (1,)), mine_reduce, other_reduce]).astype(jnp.int32)

    def pick(buffer, index):
        return lax.dynamic_index_in_dim(buffer, index, 0, keepdims=False)

    small_all = jnp.stack([pick(got_small, mine_gather[d]).reshape(-1) for d in range(shards)])
    pieces = []
    begin = 0
    for size in sizes:
        pieces.append(small_all[:, begin : begin + size].reshape(-1))
        begin += size
    g_first, s_first, g_second, s_second, b_out, b_down, b_qv, b_fc, w_score = pieces
    g_first, s_first, g_second, s_second, b_out, b_down = (
        part.astype(F32).reshape(1, width) for part in (g_first, s_first, g_second, s_second, b_out, b_down)
    )
    w_score = jnp.pad(w_score.reshape(width, heads), ((0, 0), (0, LANES - heads)))
    b_qkv = jnp.stack([b_qv[:width], jnp.zeros((width,), b_qv.dtype), b_qv[width:]]).astype(F32).reshape(3, 1, width)

    x_tail = net.shifted(block_input[:, blocks - WINDOW :], 1).reshape(tail, width)

    def halves(value, axis):
        size = value.shape[axis] // 2
        first = lax.slice_in_dim(value, 0, size, axis=axis)
        second = lax.slice_in_dim(value, size, 2 * size, axis=axis)
        return first, second

    def gathered(first, second):
        own = jnp.where(core == 0, first, second)
        mine = net.gather(own)
        other = net.chip(mine)
        mine = jnp.stack([pick(mine, mine_gather[d]) for d in range(shards)])
        other = jnp.stack([pick(other, other_gather[d]) for d in range(shards)])
        return jnp.where(core == 0, mine, other), jnp.where(core == 0, other, mine)

    qkv_blocks = jnp.transpose(qkv_weight.reshape(rows, 3, width), (1, 0, 2))
    half_rows = rows // 2
    first, second = halves(qkv_blocks, 1)
    first, second = gathered(first.reshape(3 * half_rows, width), second.reshape(3 * half_rows, width))

    def joined_blocks(first, second, count):
        both = jnp.stack([part.reshape(shards, count, half_rows, width) for part in (first, second)], axis=2)
        return jnp.transpose(both, (1, 0, 2, 3, 4)).reshape(count, width, width)

    w_qkv = joined_blocks(first, second, 3)

    deep = hidden // shards // CHUNKS
    fc_parts = fc_weight.reshape(rows, BLOCKS, shards // BLOCKS, CHUNKS, deep)
    down_parts = down_weight.reshape(CHUNKS, deep, width)
    bias_parts = b_fc.astype(F32).reshape(BLOCKS, shards // BLOCKS, CHUNKS, deep)
    out_first, out_second = halves(out_weight, 0)
    feeds = []
    w_out = None
    for chunk in range(CHUNKS):
        fc = jnp.transpose(fc_parts[:, :, :, chunk], (1, 0, 2, 3)).reshape(BLOCKS * rows, width)
        down = down_parts[chunk]
        if chunk == 0:
            fc = jnp.concatenate([fc, out_first], axis=0)
            down = jnp.concatenate([down, out_second], axis=0)
        fc, down = gathered(fc, down)
        if chunk == 0:
            main = BLOCKS * rows
            w_out = joined_blocks(fc[:, main:], down[:, main:], 1)[0]
            fc, down = fc[:, :main], down[:, :main]
        fc = jnp.transpose(fc.reshape(shards, BLOCKS, rows, width), (1, 0, 2, 3)).reshape(BLOCKS, width, width)
        down = down.reshape(BLOCKS, width, width)
        feeds.append((fc, down, bias_parts[:, :, chunk].reshape(BLOCKS, 1, width)))

    by_seq = lambda rows_, cols: pl.BlockSpec((rows_, cols), lambda s, *_: (s, 0))
    by_layer = lambda count, rows_, cols: pl.BlockSpec((count, rows_, cols), lambda s, *_: (0, s, 0))
    stat = pl.BlockSpec((1, 8, LANES), lambda s, *_: (s, 0, 0))
    shape = jax.ShapeDtypeStruct
    normed, normed_tail, importance, mass, stats = call(
        prep_kernel,
        "prep",
        (seqs,),
        [by_seq(blocks, width), by_seq(WINDOW, width), whole_spec((1, width)), whole_spec((1, width)), whole_spec((width, LANES))],
        [by_seq(blocks, width), by_seq(WINDOW, width), by_seq(blocks, LANES), by_seq(blocks, LANES), stat],
        [shape((tokens, width), BF), shape((tail, width), BF), shape((tokens, LANES), F32), shape((tokens, LANES), F32), shape((seqs, 8, LANES), F32)],
        prefetch=2,
        flops=2 * tokens * width * LANES,
        moved=2 * 2 * (tokens + tail) * width,
    )(info, bounds, x_flat, x_tail, g_first, s_first, w_score)

    peak_all, total_all = stats[:, 0], stats[:, 1]
    peak_before, total_before = jnp.full_like(peak_all, NEGATIVE), jnp.zeros_like(total_all)
    for bit in range(net.n_seq.bit_length() - 1):
        got = net.along(jnp.stack([peak_all, total_all]), bit)
        later = (net.seq >> bit) % 2 == 1
        peak_new, total_new = combine(peak_before, total_before, got[0], got[1])
        peak_before = jnp.where(later, peak_new, peak_before)
        total_before = jnp.where(later, total_new, total_before)
        peak_all, total_all = combine(peak_all, total_all, got[0], got[1])
    before = jnp.stack([peak_before, total_before, peak_all], axis=1)

    qkv, qkv_tail = call(
        qkv_kernel,
        "qkv",
        (3,),
        [whole_spec((tokens, width)), whole_spec((tail, width)), pl.BlockSpec((1, width, width), lambda j: (j, 0, 0)), pl.BlockSpec((1, 1, width), lambda j: (j, 0, 0))],
        [pl.BlockSpec((1, tokens, width), lambda j: (j, 0, 0)), pl.BlockSpec((1, tail, width), lambda j: (jnp.maximum(j - 1, 0), 0, 0))],
        [shape((3, tokens, width), BF), shape((2, tail, width), BF)],
        flops=2 * width * width * (3 * tokens + 2 * tail),
        moved=2 * width * (4 * tokens + 3 * tail + 3 * width),
    )(normed, normed_tail, w_qkv, b_qkv)

    three = pl.BlockSpec((1, 3, LANES), lambda s, *_: (s, 0, 0))
    attended, probs, gates, inverse = call(
        attention_kernel,
        "attention",
        (seqs,),
        [by_layer(3, blocks, width), by_layer(2, WINDOW, width), by_seq(blocks, LANES), by_seq(blocks, LANES), stat, three],
        [by_seq(blocks, width), by_seq(blocks, 2 * width), by_seq(WINDOW, width), by_seq(WINDOW, LANES)],
        [shape((tokens, width), BF), shape((tokens, 2 * width), BF), shape((tail, width), BF), shape((tail, LANES), F32)],
        prefetch=2,
        flops=8 * tokens * 2 * WINDOW * width,
        moved=2 * width * (7 * tokens + 3 * tail),
    )(info, bounds, qkv, qkv_tail, importance, mass, stats, before)

    tile = 2 * blocks
    by_tile = pl.BlockSpec((tile, width), lambda i, *_: (i, 0))
    middle, normed_second = call(
        project_kernel,
        "project",
        (tokens // tile,),
        [by_tile, by_tile, whole_spec((width, width)), whole_spec((1, width)), whole_spec((1, width)), whole_spec((1, width))],
        [by_tile, by_tile],
        [shape((tokens, width), F32), shape((tokens, width), BF)],
        flops=2 * tokens * width * width,
        moved=10 * tokens * width + 2 * width * width,
    )(attended, x_flat, w_out, b_out, g_second, s_second)

    block = pl.BlockSpec((1, width, width), lambda j, *_: (j, 0, 0))
    thin = pl.BlockSpec((1, 1, width), lambda j, *_: (j, 0, 0))
    full = whole_spec((tokens, width))
    chunk_rows = BLOCKS * rows
    bucket = whole_spec((shards, chunk_rows, width))
    sums_so_far = ()
    buckets = []
    d_fc_bias = []
    for chunk in range(CHUNKS):
        fc, down, bias = feeds[chunk]
        sums_so_far_specs = [full] * len(sums_so_far)
        out_sum, d_second, keep, give, d_bias = call(
            lambda *refs, first=(chunk == 0): feed_kernel(*refs, heads_in=not first),
            "feed",
            (BLOCKS,),
            [full, full, block, block, thin] + sums_so_far_specs,
            [full, full, bucket, bucket, thin],
            [shape((tokens, width), F32), shape((tokens, width), F32), shape((shards, chunk_rows, width), BF), shape((shards, chunk_rows, width), BF), shape((BLOCKS, 1, width), F32)],
            prefetch=1,
            flops=12 * tokens * width * width * BLOCKS,
            moved=2 * width * (2 * tokens + 8 * width) + 12 * tokens * width,
        )(order, normed_second, dy, fc, down, bias, *sums_so_far)
        sums_so_far = (out_sum, d_second)
        buckets.append((keep, give))
        d_fc_bias.append(d_bias.reshape(BLOCKS, shards // BLOCKS, 1, deep))
    out_sum, d_second = sums_so_far

    out_bucket = whole_spec((shards, half_rows, width))
    block_output, d_middle, d_attended, keep_out, give_out, sums_second = call(
        middle_kernel,
        "middle",
        (tokens // tile,),
        [by_tile, by_tile, by_tile, by_tile, by_tile, whole_spec((width, width)), whole_spec((1, width)), whole_spec((1, width))],
        [by_tile, by_tile, by_tile, out_bucket, out_bucket, whole_spec((8, width))],
        [shape((tokens, width), BF), shape((tokens, width), F32), shape((tokens, width), BF), shape((shards, half_rows, width), BF), shape((shards, half_rows, width), BF), shape((8, width), F32)],
        scratch=[pltpu.VMEM((width, width), F32)],
        prefetch=1,
        flops=4 * tokens * width * width,
        moved=22 * tokens * width,
    )(order, d_second, middle, dy, out_sum, attended, w_out, g_second, b_down)

    dqkv, d_halo, d_imp, totals = call(
        attention_back_kernel,
        "attention_back",
        (seqs,),
        [by_layer(3, blocks, width), by_layer(2, WINDOW, width), by_seq(blocks, width), by_seq(blocks, width), by_seq(blocks, 2 * width), by_seq(WINDOW, width), by_seq(WINDOW, LANES), by_seq(blocks, LANES), three],
        [by_layer(3, blocks, width), by_layer(2, WINDOW, width), by_seq(blocks, LANES), pl.BlockSpec((1, 1, LANES), lambda s, *_: (s, 0, 0))],
        [shape((3, tokens, width), BF), shape((2, tail, width), BF), shape((tokens, LANES), F32), shape((seqs, 1, LANES), F32)],
        scratch=[pltpu.VMEM((LANES, LANES), F32)],
        prefetch=2,
        flops=16 * tokens * 2 * WINDOW * width,
        moved=2 * width * (10 * tokens + 5 * tail),
    )(info, bounds, qkv, qkv_tail, attended, d_attended, probs, gates, inverse, importance, before)

    total_all = totals
    total_after = jnp.zeros_like(totals)
    for bit in range(net.n_seq.bit_length() - 1):
        got = net.along(total_all, bit)
        earlier = (net.seq >> bit) % 2 == 0
        total_after = jnp.where(earlier, total_after + got, total_after)
        total_all = total_all + got

    d_tail, sums_tail = call(
        tail_back_kernel,
        "tail_back",
        (1,),
        [whole_spec((2, tail, width)), whole_spec((3, width, width)), whole_spec((tail, width)), whole_spec((1, width))],
        [whole_spec((tail, width)), whole_spec((8, width))],
        [shape((tail, width), BF), shape((8, width), F32)],
        flops=4 * tail * width * width,
        moved=2 * width * (4 * tail + 3 * width),
    )(d_halo, w_qkv, x_tail, g_first)
    back = net.shifted(d_tail, -1).reshape(seqs, WINDOW, width)

    qkv_bucket = whole_spec((shards, 3 * half_rows, width))
    keep_qkv, give_qkv, sums_qkv = call(
        qkv_grad_kernel,
        "qkv_grad",
        (3,),
        [full, whole_spec((tail, width)), pl.BlockSpec((1, tokens, width), lambda j, *_: (j, 0, 0)), pl.BlockSpec((1, tail, width), lambda j, *_: (jnp.maximum(j - 1, 0), 0, 0))],
        [qkv_bucket, qkv_bucket, thin],
        [shape((shards, 3 * half_rows, width), BF), shape((shards, 3 * half_rows, width), BF), shape((3, 1, width), F32)],
        prefetch=1,
        flops=2 * width * width * (3 * tokens + 2 * tail),
        moved=2 * width * (4 * tokens + 3 * tail + 3 * width),
    )(order, normed, normed_tail, dqkv, d_halo)

    per_tile = tile // blocks
    input_grad, sums_first, d_score = call(
        input_grad_kernel,
        "input_grad",
        (tokens // tile,),
        [
            pl.BlockSpec((3, tile, width), lambda i, *_: (0, i, 0)),
            whole_spec((3, width, width)),
            whole_spec((width, LANES)),
            by_tile,
            by_tile,
            whole_spec((1, width)),
            by_tile,
            pl.BlockSpec((per_tile, WINDOW, width), lambda i, *_: (i, 0, 0)),
            pl.BlockSpec((tile, LANES), lambda i, *_: (i, 0)),
            pl.BlockSpec((tile, LANES), lambda i, *_: (i, 0)),
            pl.BlockSpec((per_tile, 3, LANES), lambda i, *_: (i, 0, 0)),
            pl.BlockSpec((per_tile, 1, LANES), lambda i, *_: (i, 0, 0)),
        ],
        [by_tile, whole_spec((8, width)), whole_spec((width, LANES))],
        [shape((tokens, width), F32), shape((8, width), F32), shape((width, LANES), F32)],
        prefetch=2,
        flops=6 * tokens * width * width,
        moved=20 * tokens * width + 6 * width * width,
    )(info, bounds, dqkv, w_qkv, w_score, normed, x_flat, g_first, d_middle, back, d_imp, importance, before, total_after)

    def chip_sum(keep, give):
        return add(keep, net.chip(give))

    def split_cores(mine):
        other = net.chip(mine)
        return jnp.where(core == 0, mine, other), jnp.where(core == 0, other, mine)

    d_fc, d_down = [], []
    fc, down = split_cores(net.reduce(chip_sum(*buckets[0])))
    d_fc.append(fc)
    d_down.append(down)
    late = jnp.concatenate([chip_sum(*buckets[1]), chip_sum(keep_out, give_out)], axis=1)
    fc, down = split_cores(net.reduce(late))
    d_fc.append(fc[:chunk_rows])
    d_down.append(down[:chunk_rows])
    d_out = jnp.concatenate([fc[chunk_rows:], down[chunk_rows:]], axis=0).astype(F32)
    first, second = split_cores(net.reduce(chip_sum(keep_qkv, give_qkv)))
    d_qkv = jnp.stack([part.reshape(3, half_rows, width) for part in (first, second)], axis=1)
    d_qkv = jnp.transpose(d_qkv.reshape(3, rows, width), (1, 0, 2)).reshape(rows, 3 * width).astype(F32)
    d_fc = jnp.stack([part.reshape(BLOCKS, rows, shards // BLOCKS, deep) for part in d_fc], axis=3)
    d_fc = jnp.transpose(d_fc, (1, 0, 2, 3, 4)).reshape(rows, hidden).astype(F32)
    d_down = jnp.stack(d_down).reshape(hidden // shards, width).astype(F32)

    d_fc_bias = jnp.concatenate(d_fc_bias, axis=2).reshape(-1)
    small_grads = [
        sums_first[0] + sums_tail[0],
        sums_first[1] + sums_tail[1],
        sums_second[0],
        sums_second[1],
        sums_second[2],
        sums_second[3],
        jnp.concatenate([sums_qkv[0, 0], sums_qkv[2, 0]]),
        d_fc_bias,
        d_score[:, :heads].reshape(-1),
    ]
    packed = jnp.concatenate([part.reshape(shards, -1) for part in small_grads], axis=1)
    packed = net.sum_all(packed)
    packed = lax.dynamic_index_in_dim(packed, net.dp, 0, keepdims=False)
    outs = []
    begin = 0
    for size in sizes:
        outs.append(packed[begin : begin + size])
        begin += size
    dg_first, ds_first, dg_second, ds_second, db_out, db_down, db_qv, db_fc, d_score = outs
    return (
        block_output.reshape(seqs, blocks, width),
        input_grad.reshape(seqs, blocks, width),
        dg_first,
        ds_first,
        d_qkv,
        db_qv,
        d_score.reshape(rows, heads),
        d_out,
        db_out,
        dg_second,
        ds_second,
        d_fc,
        db_fc,
        d_down,
        db_down,
    )


def solution(mesh):
    split = P("dp", "seq", None)
    rows = P("dp", None)
    flat = P("dp")
    in_specs = (split, rows, flat, flat, rows, flat, rows, rows, flat, flat, flat, rows, flat, rows, flat, split)
    out_specs = (split, split, flat, flat, rows, flat, rows, rows, flat, flat, flat, rows, flat, rows, flat)
    return jax.shard_map(body, mesh=mesh, in_specs=in_specs, out_specs=out_specs, check_vma=False)
```

time: 701 us -> 417 us (0.59)
  blocking collectives: 186 us -> 0 us
  matrix products: 161 us -> 0 us
  Pallas kernels: 0 us -> 146 us
  waiting for transfers between devices: 167 us -> 108 us
  starting transfers between devices: 16.7 us -> 58.6 us
  local copies, waits for them, and re-layouts: 77.7 us -> 42.9 us
  other arithmetic: 65.8 us -> 36.8 us
    dot_general x46 -> x0, matrix products: 161 us -> none  [the longest x2 18.9 us: body(): jnp.dot(run_hidden, run_w_down, preferred_element_type=jnp.float32)]
    pallas_call x0 -> x11, Pallas kernels: none -> 146 us  [the longest x2 52.5 us: body(): call(lambda *refs, first=chunk == 0: feed_kernel(*refs, heads_in=not firs...]
    reduce_scatter x4 -> x0, waiting for transfers between devices: 129 us -> none  [the longest x1 60.1 us: body(): lax.psum_scatter(totals[9].astype(jnp.bfloat16), 'dp', scatter_dimension=...]
    ppermute x8 -> x46, waiting for transfers between devices: 0.02 us -> 108 us  [send(): return lax.ppermute(value, ('seq', 'dp'), pairs)]
    all_gather x9 -> x0, blocking collectives: 107 us -> none  [the longest x6 84.5 us: prefix(): pieces = jax.tree.map(lambda part: lax.all_gather(part, axis), value)]
    unnamed x3 -> x0, blocking collectives: 47.7 us -> none
    ppermute x8 -> x46, starting transfers between devices: 15.5 us -> 58.6 us  [send(): return lax.ppermute(value, ('seq', 'dp'), pairs)]
    psum x1 -> x0, waiting for transfers between devices: 35.1 us -> none  [body(): lax.psum(totals[2].astype(jnp.bfloat16), 'seq').astype(jnp.float32)]
  transfers between devices with their start and end apart: 18 -> 46, of which waited for: 4 -> 23; matrix products, arithmetic and copies ran while one was open for 34% -> 13% of each run, Pallas kernels for 0% -> 28%
where the time goes in v1:
time: 417 us; the launch traced here: 410 us
  Pallas kernels  146 us (35%)
  waiting for transfers between devices  108 us (26%)
  starting transfers between devices  58.6 us (14%)
  local copies, waits for them, and re-layouts  42.9 us (10%)
  other arithmetic  36.8 us (9%)
  between operations  17.7 us (4%)
    ppermute x46, waiting for transfers between devices, send(): return lax.ppermute(value, ('seq', 'dp'), pairs)  108 us
    ppermute x46, starting transfers between devices, send(): return lax.ppermute(value, ('seq', 'dp'), pairs)  58.6 us
    pallas_call x2, Pallas kernels, body(): call(lambda *refs, first=chunk == 0: feed_kernel(*refs, heads_in=not firs...  52.5 us
    pallas_call x1, Pallas kernels, body(): call(attention_back_kernel, 'attention_back', (seqs,), [by_layer(3, block...  16 us
    pallas_call x1, Pallas kernels, body(): call(attention_kernel, 'attention', (seqs,), [by_layer(3, blocks, width),...  13 us
    pallas_call x1, Pallas kernels, body(): call(middle_kernel, 'middle', (tokens // tile,), [by_tile, by_tile, by_ti...  12.1 us
    pallas_call x1, Pallas kernels, body(): call(input_grad_kernel, 'input_grad', (tokens // tile,), [pl.BlockSpec((3...  12 us
    pallas_call x1, Pallas kernels, body(): call(qkv_grad_kernel, 'qkv_grad', (3,), [full, whole_spec((tail, width)),...  11.5 us
  transfers between devices with their start and end apart: 46, of which 23 were waited for; matrix products, arithmetic and copies ran while one was open for 13% of the time, Pallas kernels for 28%

profile of v1, /device:TPU:0, one launch (start us, length us, event | category | flops | bytes accessed | tf_op | source)
XLA Modules:
  0.0 410.4 jit_solution(3002444387613045428)
XLA Ops:
  51.9 8.6 %prep.1 = (bf16[1024,768]{1,0:T(8,128)(2,1)}, bf16[512,768]{1,0:T(8,128)(2,1)}, f32[1024,128]{1,0:T(8,128)}, f32[1024,128]{1,0:T(8,128)}, f32[8,8,128]{2,1,0:T(8,128)}) custom-call(s32[1]{0:T(128)} %bitcast.1.info, s32[16]{0:T(128)} %reshape.777.bounds, bf16[1024,768]{1,0:T(8,128)(2,1)} %bitcast.164, bf16[512,768]{1,0:T(8,128)(2,1)} %bitcast.3.tail_ref.x_ref, ...), custom_call_target="tpu_custom_call" | custom-call | flops 201326592 | bytes 4718592 | tf_op jit(solution)/shard_map/prep/pallas_call | solution.py:660
  73.6 14.1 %collective-permute-done.10 = bf16[2,480,768]{2,1,0:T(8,128)(2,1)} collective-permute-done((bf16[2,480,768]{2,1,0:T(8,128)(2,1)}, bf16[2,480,768]{2,1,0:T(8,128)(2,1)}, u32[]{:S(2)}, u32[]{:S(2)}) %collective-permute-start.10) | collective-permute-done | bytes 1474592 | tf_op jit(solution)/shard_map/ppermute | solution.py:494
  95.1 9.2 %qkv.1 = (bf16[3,1024,768]{2,1,0:T(8,128)(2,1)}, bf16[2,512,768]{2,1,0:T(8,128)(2,1)}) custom-call(bf16[1024,768]{1,0:T(8,128)(2,1)} %get-tuple-element.56.normed_ref, bf16[512,768]{1,0:T(8,128)(2,1)} %get-tuple-element.57.tail_ref, bf16[3,768,768]{2,1,0:T(8,128)(2,1)} %bitcast.161, f32[3,1,768]{2,1,0:T(1,128)} %maximum_convert_fusion.1.bias_ref), custom_call_target="tpu_custom_call" | custom-call | flops 4831838208 | bytes 12189696 | tf_op jit(solution)/shard_map/qkv/pallas_call | solution.py:683
  104.4 13.0 %attention.1 = (bf16[1024,768]{1,0:T(8,128)(2,1)}, bf16[1024,1536]{1,0:T(8,128)(2,1)}, bf16[512,768]{1,0:T(8,128)(2,1)}, f32[512,128]{1,0:T(8,128)}) custom-call(s32[1]{0:T(128)} %bitcast.1.info, s32[16]{0:T(128)} %reshape.777.bounds, bf16[3,1024,768]{2,1,0:T(8,128)(2,1)} %get-tuple-element.58.qkv_ref, bf16[2,512,768]{2,1,0:T(8,128)(2,1)} %get-tuple-element.59.halo_ref, ...), custom_call_target="tpu_custom_call" | custom-call | flops 805306368 | bytes 13369344 | tf_op jit(solution)/shard_map/attention/pallas_call | solution.py:695
  130.7 5.8 %project.1 = (f32[1024,768]{1,0:T(8,128)}, bf16[1024,768]{1,0:T(8,128)(2,1)}) custom-call(bf16[1024,768]{1,0:T(8,128)(2,1)} %get-tuple-element.63.att_ref, bf16[1024,768]{1,0:T(8,128)(2,1)} %bitcast.165, bf16[768,768]{1,0:T(8,128)(2,1)} %bitcast.177, f32[1,768]{1,0:T(1,128)} %reshape.798.bias_ref, f32[1,768]{1,0:T(1,128)} %reshape.799.gain_ref, ...), custom_call_target="tpu_custom_call" | custom-call | flops 1207959552 | bytes 9043968 | tf_op jit(solution)/shard_map/project/pallas_call | solution.py:709
  136.6 25.4 %feed.2 = (f32[1024,768]{1,0:T(8,128)}, f32[1024,768]{1,0:T(8,128)}, bf16[4,384,768]{2,1,0:T(8,128)(2,1)}, bf16[4,384,768]{2,1,0:T(8,128)(2,1)}, f32[2,1,768]{2,1,0:T(1,128)}) custom-call(s32[9]{0:T(128)} %pad_add_fusion.refs_0_.order, bf16[1024,768]{1,0:T(8,128)(2,1)} %get-tuple-element.64.refs_1_, bf16[1024,768]{1,0:T(8,128)(2,1)} %bitcast.200, ...), custom_call_target="tpu_custom_call" | custom-call | flops 14495514624 | bytes 22020096 | tf_op jit(solution)/shard_map/feed/pallas_call | solution.py:731
  162.4 27.1 %feed.3 = (f32[1024,768]{1,0:T(8,128)}, f32[1024,768]{1,0:T(8,128)}, bf16[4,384,768]{2,1,0:T(8,128)(2,1)}, bf16[4,384,768]{2,1,0:T(8,128)(2,1)}, f32[2,1,768]{2,1,0:T(1,128)}) custom-call(s32[9]{0:T(128)} %pad_add_fusion.refs_0_.order, bf16[1024,768]{1,0:T(8,128)(2,1)} %get-tuple-element.64.refs_1_, bf16[1024,768]{1,0:T(8,128)(2,1)} %bitcast.201, ...), custom_call_target="tpu_custom_call" | custom-call | flops 14495514624 | bytes 22020096 | tf_op jit(solution)/shard_map/feed/pallas_call | solution.py:731
  189.6 12.1 %middle.1 = (bf16[1024,768]{1,0:T(8,128)(2,1)}, f32[1024,768]{1,0:T(8,128)}, bf16[1024,768]{1,0:T(8,128)(2,1)}, bf16[4,96,768]{2,1,0:T(8,128)(2,1)}, bf16[4,96,768]{2,1,0:T(8,128)(2,1)}, /*index=5*/f32[8,768]{1,0:T(8,128)}) custom-call(s32[9]{0:T(128)} %pad_add_fusion.refs_0_.order, f32[1024,768]{1,0:T(8,128)} %get-tuple-element.67.dsec_ref, ...), custom_call_target="tpu_custom_call" | custom-call | flops 2415919104 | bytes 17301504 | tf_op jit(solution)/shard_map/middle/pallas_call | solution.py:748
  202.3 16.0 %attention_back.1 = (bf16[3,1024,768]{2,1,0:T(8,128)(2,1)}, bf16[2,512,768]{2,1,0:T(8,128)(2,1)}, f32[1024,128]{1,0:T(8,128)}, f32[8,1,128]{2,1,0:T(1,128)}) custom-call(s32[1]{0:T(128)} %bitcast.1.info, s32[16]{0:T(128)} %reshape.777.bounds, bf16[3,1024,768]{2,1,0:T(8,128)(2,1)} %get-tuple-element.58.qkv_ref, ...), custom_call_target="tpu_custom_call" | custom-call | flops 1610612736 | bytes 19660800 | tf_op jit(solution)/shard_map/attention_back/pallas_call | solution.py:761
  218.3 5.5 %tail_back.1 = (bf16[512,768]{1,0:T(8,128)(2,1)}, f32[8,768]{1,0:T(8,128)}) custom-call(bf16[2,512,768]{2,1,0:T(8,128)(2,1)} %get-tuple-element.77.dhalo_ref, bf16[3,768,768]{2,1,0:T(8,128)(2,1)} %bitcast.162, bf16[512,768]{1,0:T(8,128)(2,1)} %bitcast.3.tail_ref.x_ref, f32[1,768]{1,0:T(1,128)} %reshape.796.gain_ref), custom_call_target="tpu_custom_call" | custom-call | flops 1207959552 | bytes 6684672 | tf_op jit(solution)/shard_map/tail_back/pallas_call | solution.py:782
  225.1 11.5 %qkv_grad.1 = (bf16[4,288,768]{2,1,0:T(8,128)(2,1)}, bf16[4,288,768]{2,1,0:T(8,128)(2,1)}, f32[3,1,768]{2,1,0:T(1,128)}) custom-call(s32[9]{0:T(128)} %pad_add_fusion.refs_0_.order, bf16[1024,768]{1,0:T(8,128)(2,1)} %get-tuple-element.56.normed_ref, bf16[512,768]{1,0:T(8,128)(2,1)} %get-tuple-element.57.tail_ref, ...), custom_call_target="tpu_custom_call" | custom-call | flops 4831838208 | bytes 12189696 | tf_op jit(solution)/shard_map/qkv_grad/pallas_call | solution.py:795
  247.5 12.0 %input_grad.1 = (f32[1024,768]{1,0:T(8,128)}, f32[8,768]{1,0:T(8,128)}, f32[768,128]{1,0:T(8,128)}) custom-call(s32[1]{0:T(128)} %bitcast.1.info, s32[16]{0:T(128)} %reshape.777.bounds, bf16[3,1024,768]{2,1,0:T(8,128)(2,1)} %get-tuple-element.75.dqkv_ref, bf16[3,768,768]{2,1,0:T(8,128)(2,1)} %bitcast.163, bf16[768,128]{1,0:T(8,128)(2,1)} %pad.4.score_ref, ...), custom_call_target="tpu_custom_call" | custom-call | flops 3623878656 | bytes 19267584 | tf_op jit(solution)/shard_map/input_grad/pallas_call | solution.py:808
  268.4 3.9 collective-permute-done.21
  292.3 7.7 %collective-permute-done.25 = bf16[2,288,768]{2,1,0:T(8,128)(2,1)S(1)} collective-permute-done((bf16[2,288,768]{2,1,0:T(8,128)(2,1)S(1)}, bf16[2,288,768]{2,1,0:T(8,128)(2,1)S(1)}, u32[]{:S(2)}, u32[]{:S(2)}) %collective-permute-start.25) | collective-permute-done | bytes 884768 | tf_op jit(solution)/shard_map/ppermute | solution.py:494
  302.6 10.8 %collective-permute-done.26 = bf16[1,288,768]{2,1,0:T(8,128)(2,1)S(1)} collective-permute-done((bf16[1,288,768]{2,1,0:T(8,128)(2,1)S(1)}, bf16[1,288,768]{2,1,0:T(8,128)(2,1)S(1)}, u32[]{:S(2)}, u32[]{:S(2)}) %collective-permute-start.26) | collective-permute-done | bytes 442400 | tf_op jit(solution)/shard_map/ppermute | solution.py:494
  320.6 4.0 collective-permute-start.28
  324.6 16.5 %collective-permute-done.33 = bf16[2,480,768]{2,1,0:T(8,128)(2,1)S(1)} collective-permute-done((bf16[2,480,768]{2,1,0:T(8,128)(2,1)S(1)}, bf16[2,480,768]{2,1,0:T(8,128)(2,1)S(1)}, u32[]{:S(2)}, u32[]{:S(2)}) %collective-permute-start.33) | collective-permute-done | bytes 1474592 | tf_op jit(solution)/shard_map/ppermute | solution.py:494
  345.5 7.5 %collective-permute-done.34 = bf16[1,480,768]{2,1,0:T(8,128)(2,1)S(1)} collective-permute-done((bf16[1,480,768]{2,1,0:T(8,128)(2,1)S(1)}, bf16[1,480,768]{2,1,0:T(8,128)(2,1)S(1)}, u32[]{:S(2)}, u32[]{:S(2)}) %collective-permute-start.34) | collective-permute-done | bytes 737312 | tf_op jit(solution)/shard_map/ppermute | solution.py:494
  358.7 3.7 collective-permute-start.43
  363.5 4.1 collective-permute-start.36
  367.6 13.8 %collective-permute-done.43 = bf16[192,768]{1,0:T(8,128)(2,1)S(1)} collective-permute-done((bf16[192,768]{1,0:T(8,128)(2,1)S(1)}, bf16[192,768]{1,0:T(8,128)(2,1)S(1)}, u32[]{:S(2)}, u32[]{:S(2)}) %collective-permute-start.43) | collective-permute-done | bytes 294944 | tf_op jit(solution)/shard_map/ppermute | solution.py:494
  382.2 4.0 collective-permute-done.36
  386.8 5.6 %collective-permute-done.44 = bf16[192,768]{1,0:T(8,128)(2,1)S(1)} collective-permute-done((bf16[192,768]{1,0:T(8,128)(2,1)S(1)}, bf16[192,768]{1,0:T(8,128)(2,1)S(1)}, u32[]{:S(2)}, u32[]{:S(2)}) %collective-permute-start.44) | collective-permute-done | bytes 294944 | tf_op jit(solution)/shard_map/ppermute | solution.py:494
  392.5 4.6 %collective-permute-done.37 = bf16[240,768]{1,0:T(8,128)(2,1)S(1)} collective-permute-done((bf16[240,768]{1,0:T(8,128)(2,1)S(1)}, bf16[240,768]{1,0:T(8,128)(2,1)S(1)}, u32[]{:S(2)}, u32[]{:S(2)}) %collective-permute-start.37) | collective-permute-done | bytes 368672 | tf_op jit(solution)/shard_map/ppermute | solution.py:494
  (293 shorter events, 146.3 us)
Async XLA Ops:
  9.1 40.0 %collective-permute-start.9 = (bf16[1,480,768]{2,1,0:T(8,128)(2,1)S(1)}, bf16[1,480,768]{2,1,0:T(8,128)(2,1)}, u32[]{:S(2)}, u32[]{:S(2)}) collective-permute-start(bf16[1,480,768]{2,1,0:T(8,128)(2,1)S(1)} %maximum_select_fusion.2), channel_id=1, source_target_pairs={{0,1},{1,0},{2,3},{3,2},{4,6},{5,7},{6,4},{7,5},{8,9},{9,8},{10,11... | collective-permute-start | bytes 2211848 | tf_op jit(solution)/shard_map/ppermute | solution.py:494
  13.8 38.2 %collective-permute-start = (bf16[8,64,768]{2,1,0:T(8,128)(2,1)}, bf16[8,64,768]{2,1,0:T(8,128)(2,1)}, u32[]{:S(2)}, u32[]{:S(2)}) collective-permute-start(bf16[8,64,768]{2,1,0:T(8,128)(2,1)} %slice.314), channel_id=1, source_target_pairs={{0,4},{1,5},{2,6},{3,7},{4,8},{5,9},{6,10},{7,11},{8,12},{9,13},{1... | collective-permute-start | bytes 2359304 | tf_op jit(solution)/shard_map/ppermute | solution.py:494
  18.9 26.1 %collective-permute-start.3 = (bf16[1,288,768]{2,1,0:T(8,128)(2,1)S(1)}, bf16[1,288,768]{2,1,0:T(8,128)(2,1)S(1)}, u32[]{:S(2)}, u32[]{:S(2)}) collective-permute-start(bf16[1,288,768]{2,1,0:T(8,128)(2,1)S(1)} %bitcast.179), channel_id=1, source_target_pairs={{0,1},{1,0},{2,3},{3,2},{4,6},{5,7},{6,4},{7,5},{8,9},{9,8},{10,11... | collective-permute-start | bytes 1327112 | tf_op jit(solution)/shard_map/ppermute | solution.py:494
  20.5 26.0 %collective-permute-start.12 = (bf16[1,384,768]{2,1,0:T(8,128)(2,1)S(1)}, bf16[1,384,768]{2,1,0:T(8,128)(2,1)S(1)}, u32[]{:S(2)}, u32[]{:S(2)}) collective-permute-start(bf16[1,384,768]{2,1,0:T(8,128)(2,1)S(1)} %get-tuple-element.154), channel_id=1, source_target_pairs={{0,1},{1,0},{2,3},{3,2},{4,6},{5,7},{6,4},{7,5},{8,9},{9,8},{10,11... | collective-permute-start | bytes 1769480 | tf_op jit(solution)/shard_map/ppermute | solution.py:494
  22.2 18.5 %collective-permute-start.2 = (bf16[2,36,128]{2,1,0:T(8,128)(2,1)S(1)}, bf16[2,36,128]{2,1,0:T(8,128)(2,1)S(1)}, u32[]{:S(2)}, u32[]{:S(2)}) collective-permute-start(bf16[2,36,128]{2,1,0:T(8,128)(2,1)S(1)} %pad_maximum_fusion.20), channel_id=1, source_target_pairs={{0,2},{1,3},{2,0},{3,1},{4,5},{5,4},{6,7},{7,6},{8,10},{9,11},{10,... | collective-permute-start | bytes 55304 | tf_op jit(solution)/shard_map/ppermute | solution.py:494
  46.0 19.8 %collective-permute-start.4 = (bf16[2,288,768]{2,1,0:T(8,128)(2,1)}, bf16[2,288,768]{2,1,0:T(8,128)(2,1)}, u32[]{:S(2)}, u32[]{:S(2)}) collective-permute-start(bf16[2,288,768]{2,1,0:T(8,128)(2,1)} %pad_maximum_fusion.13), channel_id=1, source_target_pairs={{0,2},{1,3},{2,0},{3,1},{4,5},{5,4},{6,7},{7,6},{8,10},{9,11},{10,... | collective-permute-start | bytes 2654216 | tf_op jit(solution)/shard_map/ppermute | solution.py:494
  47.6 24.4 %collective-permute-start.13 = (bf16[2,384,768]{2,1,0:T(8,128)(2,1)}, bf16[2,384,768]{2,1,0:T(8,128)(2,1)}, u32[]{:S(2)}, u32[]{:S(2)}) collective-permute-start(bf16[2,384,768]{2,1,0:T(8,128)(2,1)} %pad_maximum_fusion.11), channel_id=1, source_target_pairs={{0,2},{1,3},{2,0},{3,1},{4,5},{5,4},{6,7},{7,6},{8,10},{9,11},{10,... | collective-permute-start | bytes 3538952 | tf_op jit(solution)/shard_map/ppermute | solution.py:494
  51.5 36.3 %collective-permute-start.10 = (bf16[2,480,768]{2,1,0:T(8,128)(2,1)}, bf16[2,480,768]{2,1,0:T(8,128)(2,1)}, u32[]{:S(2)}, u32[]{:S(2)}) collective-permute-start(bf16[2,480,768]{2,1,0:T(8,128)(2,1)} %pad_maximum_fusion.9), channel_id=1, source_target_pairs={{0,2},{1,3},{2,0},{3,1},{4,5},{5,4},{6,7},{7,6},{8,10},{9,11},{10,... | collective-permute-start | bytes 4423688 | tf_op jit(solution)/shard_map/ppermute | solution.py:494
  67.1 25.2 %collective-permute-start.5 = (bf16[4,288,768]{2,1,0:T(8,128)(2,1)S(1)}, bf16[4,288,768]{2,1,0:T(8,128)(2,1)S(1)}, u32[]{:S(2)}, u32[]{:S(2)}) collective-permute-start(bf16[4,288,768]{2,1,0:T(8,128)(2,1)S(1)} %pad_maximum_fusion.5), channel_id=1, source_target_pairs={{0,4},{1,5},{2,6},{3,7},{4,0},{5,1},{6,2},{7,3},{8,12},{9,13},{10,... | collective-permute-start | bytes 5308424 | tf_op jit(solution)/shard_map/ppermute | solution.py:494
  73.5 44.0 %collective-permute-start.14 = (bf16[4,384,768]{2,1,0:T(8,128)(2,1)S(1)}, bf16[4,384,768]{2,1,0:T(8,128)(2,1)}, u32[]{:S(2)}, u32[]{:S(2)}) collective-permute-start(bf16[4,384,768]{2,1,0:T(8,128)(2,1)S(1)} %pad_maximum_fusion.4), channel_id=1, source_target_pairs={{0,4},{1,5},{2,6},{3,7},{4,0},{5,1},{6,2},{7,3},{8,12},{9,13},{10,... | collective-permute-start | bytes 7077896 | tf_op jit(solution)/shard_map/ppermute | solution.py:494
  89.6 33.0 %collective-permute-start.11 = (bf16[4,480,768]{2,1,0:T(8,128)(2,1)S(1)}, bf16[4,480,768]{2,1,0:T(8,128)(2,1)}, u32[]{:S(2)}, u32[]{:S(2)}) collective-permute-start(bf16[4,480,768]{2,1,0:T(8,128)(2,1)S(1)} %pad_maximum_fusion.1), channel_id=1, source_target_pairs={{0,4},{1,5},{2,6},{3,7},{4,0},{5,1},{6,2},{7,3},{8,12},{9,13},{10,... | collective-permute-start | bytes 8847368 | tf_op jit(solution)/shard_map/ppermute | solution.py:494
  161.9 125.2 %collective-permute-start.39 = (bf16[4,384,768]{2,1,0:T(8,128)(2,1)}, bf16[4,384,768]{2,1,0:T(8,128)(2,1)S(1)}, u32[]{:S(2)}, u32[]{:S(2)}) collective-permute-start(bf16[4,384,768]{2,1,0:T(8,128)(2,1)} %get-tuple-element.96), channel_id=1, source_target_pairs={{0,4},{1,5},{2,6},{3,7},{4,0},{5,1},{6,2},{7,3},{8,12},{9,13},{10,... | collective-permute-start | bytes 7077896 | tf_op jit(solution)/shard_map/ppermute | solution.py:494
  189.5 98.9 %collective-permute-start.31 = (bf16[4,384,768]{2,1,0:T(8,128)(2,1)}, bf16[4,384,768]{2,1,0:T(8,128)(2,1)}, u32[]{:S(2)}, u32[]{:S(2)}) collective-permute-start(bf16[4,384,768]{2,1,0:T(8,128)(2,1)} %get-tuple-element.92), channel_id=1, source_target_pairs={{0,4},{1,5},{2,6},{3,7},{4,0},{5,1},{6,2},{7,3},{8,12},{9,13},{10,... | collective-permute-start | bytes 7077896 | tf_op jit(solution)/shard_map/ppermute | solution.py:494
  201.7 78.0 %collective-permute-start.32 = (bf16[4,96,768]{2,1,0:T(8,128)(2,1)}, bf16[4,96,768]{2,1,0:T(8,128)(2,1)}, u32[]{:S(2)}, u32[]{:S(2)}) collective-permute-start(bf16[4,96,768]{2,1,0:T(8,128)(2,1)} %get-tuple-element.94), channel_id=1, source_target_pairs={{0,4},{1,5},{2,6},{3,7},{4,0},{5,1},{6,2},{7,3},{8,12},{9,13},{10,... | collective-permute-start | bytes 1769480 | tf_op jit(solution)/shard_map/ppermute | solution.py:494
  223.8 23.7 %collective-permute-start.15 = (bf16[512,768]{1,0:T(8,128)(2,1)}, bf16[512,768]{1,0:T(8,128)(2,1)}, u32[]{:S(2)}, u32[]{:S(2)}) collective-permute-start(bf16[512,768]{1,0:T(8,128)(2,1)} %get-tuple-element.78), channel_id=1, source_target_pairs={{4,0},{5,1},{6,2},{7,3},{8,4},{9,5},{10,6},{11,7},{12,8},{13,9},{1... | collective-permute-start | bytes 2359304 | tf_op jit(solution)/shard_map/ppermute | solution.py:494
  246.9 36.1 %collective-permute-start.24 = (bf16[4,288,768]{2,1,0:T(8,128)(2,1)}, bf16[4,288,768]{2,1,0:T(8,128)(2,1)}, u32[]{:S(2)}, u32[]{:S(2)}) collective-permute-start(bf16[4,288,768]{2,1,0:T(8,128)(2,1)} %get-tuple-element.90), channel_id=1, source_target_pairs={{0,4},{1,5},{2,6},{3,7},{4,0},{5,1},{6,2},{7,3},{8,12},{9,13},{10,... | collective-permute-start | bytes 5308424 | tf_op jit(solution)/shard_map/ppermute | solution.py:494
  287.8 31.2 %collective-permute-start.40 = (bf16[2,384,768]{2,1,0:T(8,128)(2,1)S(1)}, bf16[2,384,768]{2,1,0:T(8,128)(2,1)S(1)}, u32[]{:S(2)}, u32[]{:S(2)}) collective-permute-start(bf16[2,384,768]{2,1,0:T(8,128)(2,1)S(1)} %slice.446), channel_id=1, source_target_pairs={{0,1},{1,0},{2,3},{3,2},{4,6},{5,7},{6,4},{7,5},{8,9},{9,8},{10,11... | collective-permute-start | bytes 3538952 | tf_op jit(solution)/shard_map/ppermute | solution.py:494
  291.7 49.4 %collective-permute-start.33 = (bf16[2,480,768]{2,1,0:T(8,128)(2,1)S(1)}, bf16[2,480,768]{2,1,0:T(8,128)(2,1)S(1)}, u32[]{:S(2)}, u32[]{:S(2)}) collective-permute-start(bf16[2,480,768]{2,1,0:T(8,128)(2,1)S(1)} %pad_maximum_fusion.8), channel_id=1, source_target_pairs={{0,1},{1,0},{2,3},{3,2},{4,6},{5,7},{6,4},{7,5},{8,9},{9,8},{10,11... | collective-permute-start | bytes 4423688 | tf_op jit(solution)/shard_map/ppermute | solution.py:494
  319.3 26.0 %collective-permute-start.41 = (bf16[1,384,768]{2,1,0:T(8,128)(2,1)S(1)}, bf16[1,384,768]{2,1,0:T(8,128)(2,1)S(1)}, u32[]{:S(2)}, u32[]{:S(2)}) collective-permute-start(bf16[1,384,768]{2,1,0:T(8,128)(2,1)S(1)} %slice.448), channel_id=1, source_target_pairs={{0,2},{1,3},{2,0},{3,1},{4,5},{5,4},{6,7},{7,6},{8,10},{9,11},{10,... | collective-permute-start | bytes 1769480 | tf_op jit(solution)/shard_map/ppermute | solution.py:494
  320.6 21.5 %collective-permute-start.28 = (bf16[144,768]{1,0:T(8,128)(2,1)S(1)}, bf16[144,768]{1,0:T(8,128)(2,1)S(1)}, u32[]{:S(2)}, u32[]{:S(2)}) collective-permute-start(bf16[144,768]{1,0:T(8,128)(2,1)S(1)} %fusion.3), channel_id=1, source_target_pairs={{0,16},{1,17},{2,18},{3,19},{4,20},{5,21},{6,22},{7,23},{8,24},{9,... | collective-permute-start | bytes 663560 | tf_op jit(solution)/shard_map/ppermute | solution.py:494
  342.1 20.4 %collective-permute-start.29 = (bf16[144,768]{1,0:T(8,128)(2,1)S(1)}, bf16[144,768]{1,0:T(8,128)(2,1)S(1)}, u32[]{:S(2)}, u32[]{:S(2)}) collective-permute-start(bf16[144,768]{1,0:T(8,128)(2,1)S(1)} %add_convert_fusion.12), channel_id=1, source_target_pairs={{0,8},{1,9},{2,10},{3,11},{4,12},{5,13},{6,14},{7,15},{8,0},{9,1},... | collective-permute-start | bytes 663560 | tf_op jit(solution)/shard_map/ppermute | solution.py:494
  358.7 22.6 %collective-permute-start.43 = (bf16[192,768]{1,0:T(8,128)(2,1)S(1)}, bf16[192,768]{1,0:T(8,128)(2,1)S(1)}, u32[]{:S(2)}, u32[]{:S(2)}) collective-permute-start(bf16[192,768]{1,0:T(8,128)(2,1)S(1)} %fusion.2), channel_id=1, source_target_pairs={{0,16},{1,17},{2,18},{3,19},{4,20},{5,21},{6,22},{7,23},{8,24},{9,... | collective-permute-start | bytes 884744 | tf_op jit(solution)/shard_map/ppermute | solution.py:494
  363.5 22.7 %collective-permute-start.36 = (bf16[240,768]{1,0:T(8,128)(2,1)S(1)}, bf16[240,768]{1,0:T(8,128)(2,1)S(1)}, u32[]{:S(2)}, u32[]{:S(2)}) collective-permute-start(bf16[240,768]{1,0:T(8,128)(2,1)S(1)} %fusion.1), channel_id=1, source_target_pairs={{0,16},{1,17},{2,18},{3,19},{4,20},{5,21},{6,22},{7,23},{8,24},{9,... | collective-permute-start | bytes 1105928 | tf_op jit(solution)/shard_map/ppermute | solution.py:494
  382.1 16.1 %collective-permute-start.30 = (bf16[288,768]{1,0:T(8,128)(2,1)S(1)}, bf16[288,768]{1,0:T(8,128)(2,1)S(1)}, u32[]{:S(2)}, u32[]{:S(2)}) collective-permute-start(bf16[288,768]{1,0:T(8,128)(2,1)S(1)} %pad_maximum_fusion.17), channel_id=1, source_target_pairs={{0,4},{1,5},{2,6},{3,7},{4,0},{5,1},{6,2},{7,3},{8,12},{9,13},{10,... | collective-permute-start | bytes 1327112 | tf_op jit(solution)/shard_map/ppermute | solution.py:494
  (45 other events, 293.0 us)
